TPU v7x, 32 devices: a whole 2x2x4 slice. The times are simulated.
32 devices in a mesh: lon: 4 (over y, x), lat: 8 (over z, core).
Axes of the slice: x: 2, y: 2, z: 4, core: 2. Of those that a mesh axis runs over, the one named last changes fastest.
Arguments:
- ocean_state: float32 [4, 10, 512, 1024], P(None, None, 'lat', 'lon'), may hold values from -4 to 4
- surface_height: float32 [512, 1024], P('lat', 'lon'), may hold values from -4 to 4
- zonal_transport: float32 [512, 1024], P('lat', 'lon'), may hold values from -4 to 4
- meridional_transport: float32 [512, 1024], P('lat', 'lon'), may hold values from -4 to 4
- land_mask: int32 [512, 1024], P('lat', 'lon'), may hold values 0 or 1
- levels: int32 [512, 1024], P('lat', 'lon'), may hold values from 1 to 10
Outputs:
- next_state: float32 [4, 10, 512, 1024], P(None, None, 'lat', 'lon')
- next_surface: float32 [512, 1024], P('lat', 'lon')
- next_zonal: float32 [512, 1024], P('lat', 'lon')
- next_meridional: float32 [512, 1024], P('lat', 'lon')
- streamfunction: float32 [512, 1024], P('lat', 'lon')
Inputs may be any that keep to these rules, and one draw needn't show every extreme that they name: `land_mask`: 1 marks a sea surface cell, 0 land.
All inputs are finite; a program needn't handle non-finite values. No bound on the sum of `land_mask` on one device may be relied on, other than what follows from the above.
Results may differ from a plain program's by a relative error of at most 0.0003.
Values sent between devices are 32-bit elements; how exact they have to be, the bound alone decides.
A program may use at most 64 MiB of HBM per device.

v0:
```python
import math

import jax
import jax.numpy as jnp
from jax import lax
from jax.sharding import PartitionSpec as P

NSUB = 10


eta_rate = 0.5
wave_rate = 0.8
forcing_rate = 0.1
tracer_step = 0.2
momentum_step = 0.2
diffusivity = 0.1


def partner(block, axis, stride):
    count = lax.axis_size(axis)
    route = []
    for low in range(count):
        high = low | 1 << stride
        if high != low and high < count:
            route += [(low, high), (high, low)]
    return lax.ppermute(block, axis, route)


def extended_2(cells, sides, width):
    for axis, dim in sides:
        count = lax.axis_size(axis)
        head = lax.slice_in_dim(cells, 0, width, axis=dim)
        tail = lax.slice_in_dim(cells, cells.shape[dim] - width, cells.shape[dim], axis=dim)
        cells = jnp.concatenate(
            [
                lax.ppermute(tail, axis, [(i, (i + 1) % count) for i in range(count)]),
                cells,
                lax.ppermute(head, axis, [((i + 1) % count, i) for i in range(count)]),
            ],
            axis=dim,
        )
    return cells


def passed_along(value, axis, steps):
    count = lax.axis_size(axis)
    pairs = [(source, (source + steps) % count) for source in range(count)]
    return lax.ppermute(value, axis, pairs)


def shifted(array, axis, by):
    devices = lax.axis_size(axis)
    pairs = [(i, i + by) for i in range(devices) if 0 <= i + by < devices]
    return lax.ppermute(array, axis, pairs)


def entering(value, axis, join, neutral):
    count, mine = (lax.axis_size(axis), lax.axis_index(axis))
    pieces = lax.all_gather(value, axis)
    running = jnp.full_like(value, 0) + jnp.asarray(neutral, value.dtype)

    def lap(position, running):
        longer = join(running, pieces[position])
        return jnp.where(position < mine, longer, running)

    return lax.fori_loop(0, count - 1, lap, running)


def to_middle(in_field):
    return in_field[..., 1:-1, 1:-1]


def to_east(in_field):
    return in_field[..., 1:-1, 2:]


def to_west(in_field):
    return in_field[..., 1:-1, :-2]


def to_north(in_field):
    return in_field[..., 2:, 1:-1]


def to_south(in_field):
    return in_field[..., :-2, 1:-1]


def thicknesses(level_count):
    level_index = jnp.arange(level_count, dtype=jnp.float32)
    return (level_index + 1.0) / (level_count * (level_count + 1) / 2.0)


def level_core(level_ext, carry, fields, thick_k, index_k):
    above_sum, force_x, force_y, col_depth = carry
    temper, saline, zonal_flow, merid_flow = fields
    wet_cells = (index_k < level_ext).astype(jnp.float32)
    density = (0.8 * saline - 0.3 * temper - 0.04 * temper * temper) * wet_cells
    layer_weight = density * thick_k
    pressure = above_sum + 0.5 * layer_weight
    above_sum = above_sum + layer_weight
    col_depth = col_depth + wet_cells * thick_k
    wet_mid = to_middle(wet_cells)
    wet_east = wet_mid * to_east(wet_cells)
    wet_west = wet_mid * to_west(wet_cells)
    wet_north = wet_mid * to_north(wet_cells)
    wet_south = wet_mid * to_south(wet_cells)
    grad_x = (to_east(pressure) - to_middle(pressure)) * wet_east
    grad_y = (to_north(pressure) - to_middle(pressure)) * wet_north
    u_east = to_middle(zonal_flow)
    u_west = to_west(zonal_flow)
    v_north = to_middle(merid_flow)
    v_south = to_south(merid_flow)

    def advect(tracer):
        centre = to_middle(tracer)
        flux_east = wet_east * (
            jnp.maximum(u_east, 0.0) * centre + jnp.minimum(u_east, 0.0) * to_east(tracer)
        )
        flux_west = wet_west * (
            jnp.maximum(u_west, 0.0) * to_west(tracer) + jnp.minimum(u_west, 0.0) * centre
        )
        flux_north = wet_north * (
            jnp.maximum(v_north, 0.0) * centre + jnp.minimum(v_north, 0.0) * to_north(tracer)
        )
        flux_south = wet_south * (
            jnp.maximum(v_south, 0.0) * to_south(tracer) + jnp.minimum(v_south, 0.0) * centre
        )
        mixing = diffusivity * (
            wet_east * (to_east(tracer) - centre)
            - wet_west * (centre - to_west(tracer))
            + wet_north * (to_north(tracer) - centre)
            - wet_south * (centre - to_south(tracer))
        )
        return wet_mid * (
            centre + tracer_step * (flux_west - flux_east + flux_south - flux_north + mixing)
        )

    zonal_next = wet_east * (u_east - momentum_step * grad_x)
    merid_next = wet_north * (v_north - momentum_step * grad_y)
    new_carry = (above_sum, force_x + grad_x * thick_k, force_y + grad_y * thick_k, col_depth)
    return (new_carry, (advect(temper), advect(saline), zonal_next, merid_next))


def mirror(rows_in):
    swapped = rows_in
    for bit_index in range(lax.axis_size("lon").bit_length() - 1):
        swapped = partner(swapped, "lon", bit_index)
    return jnp.flip(swapped, axis=1)


def close_rim(padded, fold_rows):
    lat_index = lax.axis_index("lat")
    top_index = lax.axis_size("lat") - 1
    north_row = jnp.pad(fold_rows, [(0, 0)] * (fold_rows.ndim - 1) + [(1, 1)])[..., None, :]
    top_rim = jnp.where(lat_index == top_index, north_row, padded[..., -1:, :])
    bottom_rim = jnp.where(lat_index == 0, jnp.zeros_like(padded[..., :1, :]), padded[..., :1, :])
    return jnp.concatenate([bottom_rim, padded[..., 1:-1, :], top_rim], axis=-2)


def add_sums(earlier, later):
    return earlier + later


def body(ocean_state, surface_height, zonal_transport, meridional_transport, land_mask, levels):
    level_count = ocean_state.shape[1]
    row_count = ocean_state.shape[2]
    col_count = ocean_state.shape[3]
    thickness = thicknesses(level_count)
    level_index = jnp.arange(level_count, dtype=jnp.float32)
    level_field = (land_mask * levels).astype(jnp.float32)
    stacked = jnp.concatenate(
        [ocean_state.reshape(4 * level_count, row_count, col_count), level_field[None]], axis=0
    )
    top_rows = jnp.concatenate(
        [
            stacked[: 2 * level_count, row_count - 1, :],
            stacked[4 * level_count :, row_count - 1, :],
        ],
        axis=0,
    )
    turned = mirror(top_rows)
    padded = extended_2(stacked, (("lon", 2), ("lat", 1)), 1)
    fold_rows = jnp.concatenate(
        [
            turned[: 2 * level_count],
            jnp.zeros((2 * level_count, col_count), jnp.float32),
            turned[2 * level_count :],
        ],
        axis=0,
    )
    extended = close_rim(padded, fold_rows)
    level_ext = extended[4 * level_count]
    state_ext = extended[: 4 * level_count].reshape(4, level_count, row_count + 2, col_count + 2)

    def per_level(carry, slices):
        temper, saline, zonal_flow, merid_flow, thick_k, index_k = slices
        return level_core(
            level_ext, carry, (temper, saline, zonal_flow, merid_flow), thick_k, index_k
        )

    start = (
        jnp.zeros((row_count + 2, col_count + 2), jnp.float32),
        jnp.zeros((row_count, col_count), jnp.float32),
        jnp.zeros((row_count, col_count), jnp.float32),
        jnp.zeros((row_count + 2, col_count + 2), jnp.float32),
    )
    carry, outputs = lax.scan(
        per_level,
        start,
        (state_ext[0], state_ext[1], state_ext[2], state_ext[3], thickness, level_index),
    )
    above_sum, force_x, force_y, col_depth = carry
    next_state = jnp.stack(list(outputs))
    depth_east = jnp.minimum(to_middle(col_depth), to_east(col_depth))
    depth_north = jnp.minimum(to_middle(col_depth), to_north(col_depth))
    surface_wet = (level_field > 0.0).astype(jnp.float32)
    open_east = (depth_east > 0.0).astype(jnp.float32)
    open_north = (depth_north > 0.0).astype(jnp.float32)
    is_top = lax.axis_index("lat") == lax.axis_size("lat") - 1
    surface = surface_height
    zonal_now = zonal_transport
    merid_now = meridional_transport
    for sub_step in range(NSUB):
        west_column = passed_along(zonal_now[:, col_count - 1 :], "lon", 1)
        south_row = shifted(merid_now[row_count - 1 :, :], "lat", 1)
        zonal_west = jnp.concatenate([west_column, zonal_now[:, : col_count - 1]], axis=1)
        merid_south = jnp.concatenate([south_row, merid_now[: row_count - 1, :]], axis=0)
        divergence = zonal_now - zonal_west + (merid_now - merid_south)
        surface = surface_wet * (surface - eta_rate * divergence)
        surface_fold = mirror(surface[row_count - 1 : row_count, :])
        east_column = passed_along(surface[:, :1], "lon", -1)
        north_row = shifted(surface[:1, :], "lat", -1)
        north_row = jnp.where(is_top, surface_fold, north_row)
        surface_east = jnp.concatenate([surface[:, 1:], east_column], axis=1)
        surface_north = jnp.concatenate([surface[1:, :], north_row], axis=0)
        zonal_now = open_east * (
            zonal_now - wave_rate * depth_east * (surface_east - surface) - forcing_rate * force_x
        )
        merid_now = open_north * (
            merid_now - wave_rate * depth_north * (surface_north - surface) - forcing_rate * force_y
        )
    local_sums = jnp.cumsum(zonal_now, axis=0)
    totals = local_sums[row_count - 1]
    below_sums = entering(totals, "lat", add_sums, jnp.zeros_like(totals))
    streamfunction = -(local_sums + below_sums[None]) / math.sqrt(row_count * lax.axis_size("lat"))
    return (next_state, surface, zonal_now, merid_now, streamfunction)


def solution(mesh):
    return jax.shard_map(
        body,
        mesh=mesh,
        in_specs=(
            P(None, None, "lat", "lon"),
            P("lat", "lon"),
            P("lat", "lon"),
            P("lat", "lon"),
            P("lat", "lon"),
            P("lat", "lon"),
        ),
        out_specs=(
            P(None, None, "lat", "lon"),
            P("lat", "lon"),
            P("lat", "lon"),
            P("lat", "lon"),
            P("lat", "lon"),
        ),
        check_vma=False,
    )
```

profile of v0, /device:TPU:0, one launch (start us, length us, event | category | flops | bytes accessed | tf_op | source)
XLA Modules:
  0.0 317.3 jit_solution(6132749015496900386)
XLA Ops:
  1.5 3.7 %fusion.5 = (f32[41,64,1]{2,1,0:T(8,128)}, f32[41,64,1]{2,1,0:T(8,128)}) fusion(f32[40,64,256]{2,1,0:T(8,128)} %bitcast.77, f32[1,64,256]{2,1,0:T(8,128)S(1)} %convert_bitcast_fusion), kind=kLoop, calls=%fused_computation.35 | loop fusion | flops 5248 | bytes 2707968 | tf_op jit(solution)/shard_map/concatenate | solution.py:172
  5.3 2.5 copy.39
  7.8 2.9 collective-permute-start
  10.8 2.4 copy.40
  16.6 2.5 collective-permute-start.3
  20.0 2.9 collective-permute-done.10
  28.0 2.3 copy.41
  30.3 2.3 copy.42
  33.3 2.2 pad_maximum_fusion.13
  35.5 5.7 %collective-permute-start.5 = (f32[41,1,258]{2,1,0:T(1,128)}, f32[41,1,258]{2,1,0:T(1,128)}, u32[]{:S(2)}, u32[]{:S(2)}) collective-permute-start(f32[41,1,258]{2,1,0:T(1,128)} %get-tuple-element.332), channel_id=1, source_target_pairs={{1,0},{2,1},{3,2},{4,3},{5,4},{6,5},{7,6},{0,7},{9,8},{10,9},{11,1... | collective-permute-start | bytes 126944 | tf_op jit(solution)/shard_map/ppermute | solution.py:38
  44.3 2.7 collective-permute-done.2
  47.1 4.7 %pad_maximum_fusion.2 = (f32[10,66,258]{2,1,0:T(8,128)}, f32[10,66,258]{2,1,0:T(8,128)}, f32[10,66,258]{2,1,0:T(8,128)}) fusion(f32[41,1,258]{2,1,0:T(1,128)S(1)} %broadcast_select_fusion, f32[41,1,258]{2,1,0:T(1,128)S(1)} %broadcast_select_fusion.1, f32[41,64,1]{2,1,0:T(8,128)} %copy.42, f32[41,64,1]{2,1,0:T(8,128)} %copy.41, ...), kind=kLoop, calls=%fused_computation.37 | loop fusion | flops 2554200 | bytes 4835952 | tf_op jit(solution)/shard_map/concatenate | solution.py:158
  53.3 92.9 %while.39 = (s32[]{:T(128)}, f32[66,258]{1,0:T(8,128)S(1)}, f32[64,256]{1,0:T(8,128)S(1)}, f32[64,256]{1,0:T(8,128)S(1)}, f32[66,258]{1,0:T(8,128)S(1)}, /*index...) while((s32[]{:T(128)}, f32[66,258]{1,0:T(8,128)S(1)}, ...), condition=%wide.region_1.2_spmd.clone, body=%wide.region_0.1_spmd.clone.sunk | while | flops 2277739 | bytes 4638230 | solution.py:208
  148.1 4.4 %collective-permute-done.9 = f32[64,1]{1,0:T(8,128)S(1)} collective-permute-done((f32[64,1]{1,0:T(8,128)S(1)}, f32[64,1]{1,0:T(8,128)S(1)}, u32[]{:S(2)}, u32[]{:S(2)}) %collective-permute-start.9) | collective-permute-done | bytes 288 | tf_op jit(solution)/shard_map/ppermute | solution.py:48
  152.8 3.6 %collective-permute-done.16 = f32[1,256]{1,0:T(1,128)S(1)} collective-permute-done((f32[1,256]{1,0:T(1,128)S(1)}, f32[1,256]{1,0:T(1,128)S(1)}, u32[]{:S(2)}, u32[]{:S(2)}) %collective-permute-start.16) | collective-permute-done | bytes 1056 | tf_op jit(solution)/shard_map/ppermute | solution.py:26
  160.9 2.5 collective-permute-done.14
  163.5 2.0 collective-permute-start.19
  166.5 3.9 %collective-permute-done.15 = f32[64,1]{1,0:T(8,128)S(1)} collective-permute-done((f32[64,1]{1,0:T(8,128)S(1)}, f32[64,1]{1,0:T(8,128)S(1)}, u32[]{:S(2)}, u32[]{:S(2)}) %collective-permute-start.15) | collective-permute-done | bytes 288 | tf_op jit(solution)/shard_map/ppermute | solution.py:48
  170.6 3.6 %collective-permute-done.22 = f32[1,256]{1,0:T(1,128)S(1)} collective-permute-done((f32[1,256]{1,0:T(1,128)S(1)}, f32[1,256]{1,0:T(1,128)S(1)}, u32[]{:S(2)}, u32[]{:S(2)}) %collective-permute-start.22) | collective-permute-done | bytes 1056 | tf_op jit(solution)/shard_map/ppermute | solution.py:26
  177.9 2.3 collective-permute-done.20
  180.3 2.0 collective-permute-start.25
  183.4 3.9 %collective-permute-done.21 = f32[64,1]{1,0:T(8,128)S(1)} collective-permute-done((f32[64,1]{1,0:T(8,128)S(1)}, f32[64,1]{1,0:T(8,128)S(1)}, u32[]{:S(2)}, u32[]{:S(2)}) %collective-permute-start.21) | collective-permute-done | bytes 288 | tf_op jit(solution)/shard_map/ppermute | solution.py:48
  187.6 3.4 %collective-permute-done.28 = f32[1,256]{1,0:T(1,128)S(1)} collective-permute-done((f32[1,256]{1,0:T(1,128)S(1)}, f32[1,256]{1,0:T(1,128)S(1)}, u32[]{:S(2)}, u32[]{:S(2)}) %collective-permute-start.28) | collective-permute-done | bytes 1056 | tf_op jit(solution)/shard_map/ppermute | solution.py:26
  195.6 2.5 collective-permute-done.26
  198.2 2.0 collective-permute-start.31
  201.2 3.9 %collective-permute-done.27 = f32[64,1]{1,0:T(8,128)S(1)} collective-permute-done((f32[64,1]{1,0:T(8,128)S(1)}, f32[64,1]{1,0:T(8,128)S(1)}, u32[]{:S(2)}, u32[]{:S(2)}) %collective-permute-start.27) | collective-permute-done | bytes 288 | tf_op jit(solution)/shard_map/ppermute | solution.py:48
  205.3 3.6 %collective-permute-done.34 = f32[1,256]{1,0:T(1,128)S(1)} collective-permute-done((f32[1,256]{1,0:T(1,128)S(1)}, f32[1,256]{1,0:T(1,128)S(1)}, u32[]{:S(2)}, u32[]{:S(2)}) %collective-permute-start.34) | collective-permute-done | bytes 1056 | tf_op jit(solution)/shard_map/ppermute | solution.py:26
  212.6 2.3 collective-permute-done.32
  218.3 3.9 %collective-permute-done.33 = f32[64,1]{1,0:T(8,128)S(1)} collective-permute-done((f32[64,1]{1,0:T(8,128)S(1)}, f32[64,1]{1,0:T(8,128)S(1)}, u32[]{:S(2)}, u32[]{:S(2)}) %collective-permute-start.33) | collective-permute-done | bytes 288 | tf_op jit(solution)/shard_map/ppermute | solution.py:48
  222.4 3.5 %collective-permute-done.40 = f32[1,256]{1,0:T(1,128)S(1)} collective-permute-done((f32[1,256]{1,0:T(1,128)S(1)}, f32[1,256]{1,0:T(1,128)S(1)}, u32[]{:S(2)}, u32[]{:S(2)}) %collective-permute-start.40) | collective-permute-done | bytes 1056 | tf_op jit(solution)/shard_map/ppermute | solution.py:26
  230.2 2.5 collective-permute-done.38
  232.9 2.0 collective-permute-start.43
  235.9 4.2 %collective-permute-done.39 = f32[64,1]{1,0:T(8,128)S(1)} collective-permute-done((f32[64,1]{1,0:T(8,128)S(1)}, f32[64,1]{1,0:T(8,128)S(1)}, u32[]{:S(2)}, u32[]{:S(2)}) %collective-permute-start.39) | collective-permute-done | bytes 288 | tf_op jit(solution)/shard_map/ppermute | solution.py:48
  240.3 3.6 %collective-permute-done.46 = f32[1,256]{1,0:T(1,128)S(1)} collective-permute-done((f32[1,256]{1,0:T(1,128)S(1)}, f32[1,256]{1,0:T(1,128)S(1)}, u32[]{:S(2)}, u32[]{:S(2)}) %collective-permute-start.46) | collective-permute-done | bytes 1056 | tf_op jit(solution)/shard_map/ppermute | solution.py:26
  247.7 2.5 collective-permute-done.44
  250.3 2.0 collective-permute-start.49
  253.2 4.3 %collective-permute-done.45 = f32[64,1]{1,0:T(8,128)S(1)} collective-permute-done((f32[64,1]{1,0:T(8,128)S(1)}, f32[64,1]{1,0:T(8,128)S(1)}, u32[]{:S(2)}, u32[]{:S(2)}) %collective-permute-start.45) | collective-permute-done | bytes 288 | tf_op jit(solution)/shard_map/ppermute | solution.py:48
  257.7 3.6 %collective-permute-done.52 = f32[1,256]{1,0:T(1,128)S(1)} collective-permute-done((f32[1,256]{1,0:T(1,128)S(1)}, f32[1,256]{1,0:T(1,128)S(1)}, u32[]{:S(2)}, u32[]{:S(2)}) %collective-permute-start.52) | collective-permute-done | bytes 1056 | tf_op jit(solution)/shard_map/ppermute | solution.py:26
  265.6 2.5 collective-permute-done.50
  268.2 2.2 collective-permute-start.55
  271.4 4.2 %collective-permute-done.51 = f32[64,1]{1,0:T(8,128)S(1)} collective-permute-done((f32[64,1]{1,0:T(8,128)S(1)}, f32[64,1]{1,0:T(8,128)S(1)}, u32[]{:S(2)}, u32[]{:S(2)}) %collective-permute-start.51) | collective-permute-done | bytes 288 | tf_op jit(solution)/shard_map/ppermute | solution.py:48
  275.8 3.6 %collective-permute-done.58 = f32[1,256]{1,0:T(1,128)S(1)} collective-permute-done((f32[1,256]{1,0:T(1,128)S(1)}, f32[1,256]{1,0:T(1,128)S(1)}, u32[]{:S(2)}, u32[]{:S(2)}) %collective-permute-start.58) | collective-permute-done | bytes 1056 | tf_op jit(solution)/shard_map/ppermute | solution.py:26
  283.2 2.5 collective-permute-done.56
  285.8 2.0 collective-permute-start.61
  288.7 4.3 %collective-permute-done.57 = f32[64,1]{1,0:T(8,128)S(1)} collective-permute-done((f32[64,1]{1,0:T(8,128)S(1)}, f32[64,1]{1,0:T(8,128)S(1)}, u32[]{:S(2)}, u32[]{:S(2)}) %collective-permute-start.57) | collective-permute-done | bytes 288 | tf_op jit(solution)/shard_map/ppermute | solution.py:48
  294.6 2.2 collective-permute-done.63
  300.6 3.3 %collective-permute-done.62 = f32[64,1]{1,0:T(8,128)S(1)} collective-permute-done((f32[64,1]{1,0:T(8,128)S(1)}, f32[64,1]{1,0:T(8,128)S(1)}, u32[]{:S(2)}, u32[]{:S(2)}) %collective-permute-start.62) | collective-permute-done | bytes 288 | tf_op jit(solution)/shard_map/ppermute | solution.py:48
  304.6 11.7 %all-gather = f32[8,1,256]{2,1,0:T(1,128)S(1)} all-gather(f32[1,1,256]{2,1,0:T(1,128)S(1)} %slice_bitcast_fusion), channel_id=1, replica_groups=mesh['lon'=4,'lat'=8] {'lat'}, dimensions={0}, use_global_device_ids=true | all-gather | bytes 9216 | tf_op jit(solution)/shard_map/all_gather | solution.py:59
  (378 shorter events, 162.0 us)
Async XLA Ops:
  7.8 20.2 %collective-permute-start = (f32[41,64,1]{1,2,0:T(1,128)}, f32[41,64,1]{1,2,0:T(1,128)}, u32[]{:S(2)}, u32[]{:S(2)}) collective-permute-start(f32[41,64,1]{1,2,0:T(1,128)} %copy.39), channel_id=1, source_target_pairs={{0,8},{8,16},{16,24},{24,0},{1,9},{9,17},{17,25},{25,1},{2,10},{10... | collective-permute-start | bytes 31496 | tf_op jit(solution)/shard_map/ppermute | solution.py:36
  13.1 17.1 %collective-permute-start.1 = (f32[41,64,1]{1,2,0:T(1,128)}, f32[41,64,1]{1,2,0:T(1,128)}, u32[]{:S(2)}, u32[]{:S(2)}) collective-permute-start(f32[41,64,1]{1,2,0:T(1,128)} %copy.40), channel_id=1, source_target_pairs={{8,0},{16,8},{24,16},{0,24},{9,1},{17,9},{25,17},{1,25},{10,2},{18... | collective-permute-start | bytes 31496 | tf_op jit(solution)/shard_map/ppermute | solution.py:38
  14.2 4.9 %collective-permute-start.6 = (f32[64,1]{1,0:T(8,128)S(1)}, f32[64,1]{1,0:T(8,128)S(1)}, u32[]{:S(2)}, u32[]{:S(2)}) collective-permute-start(f32[64,1]{1,0:T(8,128)S(1)} %slice.427), channel_id=1, source_target_pairs={{0,8},{8,16},{16,24},{24,0},{1,9},{9,17},{17,25},{25,1},{2,10},{10... | collective-permute-start | bytes 776 | tf_op jit(solution)/shard_map/ppermute | solution.py:48
  15.3 3.8 %collective-permute-start.7 = (f32[1,256]{1,0:T(1,128)S(1)}, f32[1,256]{1,0:T(1,128)S(1)}, u32[]{:S(2)}, u32[]{:S(2)}) collective-permute-start(f32[1,256]{1,0:T(1,128)S(1)} %slice.429), channel_id=1, source_target_pairs={{0,1},{1,2},{2,3},{3,4},{4,5},{5,6},{6,7},{8,9},{9,10},{10,11},{11... | collective-permute-start | bytes 3080 | tf_op jit(solution)/shard_map/ppermute | solution.py:54
  16.6 15.9 %collective-permute-start.3 = (f32[21,256]{1,0:T(8,128)S(1)}, f32[21,256]{1,0:T(8,128)}, u32[]{:S(2)}, u32[]{:S(2)}) collective-permute-start(f32[21,256]{1,0:T(8,128)S(1)} %pad_maximum_fusion.15), channel_id=1, source_target_pairs={{0,8},{8,0},{16,24},{24,16},{1,9},{9,1},{17,25},{25,17},{2,10},{10... | collective-permute-start | bytes 64520 | tf_op jit(solution)/shard_map/ppermute | solution.py:26
  19.2 3.6 %collective-permute-start.10 = (f32[1,256]{1,0:T(1,128)S(1)}, f32[1,256]{1,0:T(1,128)S(1)}, u32[]{:S(2)}, u32[]{:S(2)}) collective-permute-start(f32[1,256]{1,0:T(1,128)S(1)} %get-tuple-element.374), channel_id=1, source_target_pairs={{0,8},{8,0},{16,24},{24,16},{1,9},{9,1},{17,25},{25,17},{2,10},{10... | collective-permute-start | bytes 3080 | tf_op jit(solution)/shard_map/ppermute | solution.py:26
  22.9 4.0 %collective-permute-start.11 = (f32[1,256]{1,0:T(1,128)S(1)}, f32[1,256]{1,0:T(1,128)S(1)}, u32[]{:S(2)}, u32[]{:S(2)}) collective-permute-start(f32[1,256]{1,0:T(1,128)S(1)} %collective-permute-done.10), channel_id=1, source_target_pairs={{0,16},{16,0},{8,24},{24,8},{1,17},{17,1},{9,25},{25,9},{2,18},{18... | collective-permute-start | bytes 3080 | tf_op jit(solution)/shard_map/ppermute | solution.py:26
  26.9 119.3 %collective-permute-start.8 = (f32[64,1]{1,0:T(8,128)}, f32[64,1]{1,0:T(8,128)S(1)}, u32[]{:S(2)}, u32[]{:S(2)}) collective-permute-start(f32[64,1]{1,0:T(8,128)} %slice.572), channel_id=1, source_target_pairs={{0,24},{8,0},{16,8},{24,16},{1,25},{9,1},{17,9},{25,17},{2,26},{10... | collective-permute-start | bytes 776 | tf_op jit(solution)/shard_map/ppermute | solution.py:48
  32.5 8.7 %collective-permute-start.4 = (f32[21,256]{1,0:T(8,128)}, f32[21,256]{1,0:T(8,128)S(1)}, u32[]{:S(2)}, u32[]{:S(2)}) collective-permute-start(f32[21,256]{1,0:T(8,128)} %collective-permute-done.3), channel_id=1, source_target_pairs={{0,16},{16,0},{8,24},{24,8},{1,17},{17,1},{9,25},{25,9},{2,18},{18... | collective-permute-start | bytes 64520 | tf_op jit(solution)/shard_map/ppermute | solution.py:26
  35.5 7.9 %collective-permute-start.5 = (f32[41,1,258]{2,1,0:T(1,128)}, f32[41,1,258]{2,1,0:T(1,128)}, u32[]{:S(2)}, u32[]{:S(2)}) collective-permute-start(f32[41,1,258]{2,1,0:T(1,128)} %get-tuple-element.332), channel_id=1, source_target_pairs={{1,0},{2,1},{3,2},{4,3},{5,4},{6,5},{7,6},{0,7},{9,8},{10,9},{11,1... | collective-permute-start | bytes 126944 | tf_op jit(solution)/shard_map/ppermute | solution.py:38
  41.2 5.8 %collective-permute-start.2 = (f32[41,1,258]{2,1,0:T(1,128)}, f32[41,1,258]{2,1,0:T(1,128)}, u32[]{:S(2)}, u32[]{:S(2)}) collective-permute-start(f32[41,1,258]{2,1,0:T(1,128)} %get-tuple-element.331), channel_id=1, source_target_pairs={{0,1},{1,2},{2,3},{3,4},{4,5},{5,6},{6,7},{7,0},{8,9},{9,10},{10,1... | collective-permute-start | bytes 126944 | tf_op jit(solution)/shard_map/ppermute | solution.py:36
  146.4 6.2 %collective-permute-start.13 = (f32[1,256]{1,0:T(1,128)S(1)}, f32[1,256]{1,0:T(1,128)S(1)}, u32[]{:S(2)}, u32[]{:S(2)}) collective-permute-start(f32[1,256]{1,0:T(1,128)S(1)} %slice.578), channel_id=1, source_target_pairs={{0,1},{1,2},{2,3},{3,4},{4,5},{5,6},{6,7},{8,9},{9,10},{10,11},{11... | collective-permute-start | bytes 3080 | tf_op jit(solution)/shard_map/ppermute | solution.py:54
  147.8 4.8 %collective-permute-start.9 = (f32[64,1]{1,0:T(8,128)S(1)}, f32[64,1]{1,0:T(8,128)S(1)}, u32[]{:S(2)}, u32[]{:S(2)}) collective-permute-start(f32[64,1]{1,0:T(8,128)S(1)} %slice.573), channel_id=1, source_target_pairs={{0,8},{8,16},{16,24},{24,0},{1,9},{9,17},{17,25},{25,1},{2,10},{10... | collective-permute-start | bytes 776 | tf_op jit(solution)/shard_map/ppermute | solution.py:48
  152.7 3.6 %collective-permute-start.16 = (f32[1,256]{1,0:T(1,128)S(1)}, f32[1,256]{1,0:T(1,128)S(1)}, u32[]{:S(2)}, u32[]{:S(2)}) collective-permute-start(f32[1,256]{1,0:T(1,128)S(1)} %get-tuple-element.372), channel_id=1, source_target_pairs={{0,8},{8,0},{16,24},{24,16},{1,9},{9,1},{17,25},{25,17},{2,10},{10... | collective-permute-start | bytes 3080 | tf_op jit(solution)/shard_map/ppermute | solution.py:26
  159.2 4.2 %collective-permute-start.14 = (f32[64,1]{1,0:T(8,128)S(1)}, f32[64,1]{1,0:T(8,128)S(1)}, u32[]{:S(2)}, u32[]{:S(2)}) collective-permute-start(f32[64,1]{1,0:T(8,128)S(1)} %slice.581), channel_id=1, source_target_pairs={{0,24},{8,0},{16,8},{24,16},{1,25},{9,1},{17,9},{25,17},{2,26},{10... | collective-permute-start | bytes 776 | tf_op jit(solution)/shard_map/ppermute | solution.py:48
  163.5 6.9 %collective-permute-start.19 = (f32[1,256]{1,0:T(1,128)S(1)}, f32[1,256]{1,0:T(1,128)S(1)}, u32[]{:S(2)}, u32[]{:S(2)}) collective-permute-start(f32[1,256]{1,0:T(1,128)S(1)} %slice.587), channel_id=1, source_target_pairs={{0,1},{1,2},{2,3},{3,4},{4,5},{5,6},{6,7},{8,9},{9,10},{10,11},{11... | collective-permute-start | bytes 3080 | tf_op jit(solution)/shard_map/ppermute | solution.py:54
  165.6 4.8 %collective-permute-start.15 = (f32[64,1]{1,0:T(8,128)S(1)}, f32[64,1]{1,0:T(8,128)S(1)}, u32[]{:S(2)}, u32[]{:S(2)}) collective-permute-start(f32[64,1]{1,0:T(8,128)S(1)} %slice.582), channel_id=1, source_target_pairs={{0,8},{8,16},{16,24},{24,0},{1,9},{9,17},{17,25},{25,1},{2,10},{10... | collective-permute-start | bytes 776 | tf_op jit(solution)/shard_map/ppermute | solution.py:48
  170.5 3.6 %collective-permute-start.22 = (f32[1,256]{1,0:T(1,128)S(1)}, f32[1,256]{1,0:T(1,128)S(1)}, u32[]{:S(2)}, u32[]{:S(2)}) collective-permute-start(f32[1,256]{1,0:T(1,128)S(1)} %get-tuple-element.368), channel_id=1, source_target_pairs={{0,8},{8,0},{16,24},{24,16},{1,9},{9,1},{17,25},{25,17},{2,10},{10... | collective-permute-start | bytes 3080 | tf_op jit(solution)/shard_map/ppermute | solution.py:26
  176.1 4.2 %collective-permute-start.20 = (f32[64,1]{1,0:T(8,128)S(1)}, f32[64,1]{1,0:T(8,128)S(1)}, u32[]{:S(2)}, u32[]{:S(2)}) collective-permute-start(f32[64,1]{1,0:T(8,128)S(1)} %slice.590), channel_id=1, source_target_pairs={{0,24},{8,0},{16,8},{24,16},{1,25},{9,1},{17,9},{25,17},{2,26},{10... | collective-permute-start | bytes 776 | tf_op jit(solution)/shard_map/ppermute | solution.py:48
  180.3 6.9 %collective-permute-start.25 = (f32[1,256]{1,0:T(1,128)S(1)}, f32[1,256]{1,0:T(1,128)S(1)}, u32[]{:S(2)}, u32[]{:S(2)}) collective-permute-start(f32[1,256]{1,0:T(1,128)S(1)} %slice.596), channel_id=1, source_target_pairs={{0,1},{1,2},{2,3},{3,4},{4,5},{5,6},{6,7},{8,9},{9,10},{10,11},{11... | collective-permute-start | bytes 3080 | tf_op jit(solution)/shard_map/ppermute | solution.py:54
  182.4 4.8 %collective-permute-start.21 = (f32[64,1]{1,0:T(8,128)S(1)}, f32[64,1]{1,0:T(8,128)S(1)}, u32[]{:S(2)}, u32[]{:S(2)}) collective-permute-start(f32[64,1]{1,0:T(8,128)S(1)} %slice.591), channel_id=1, source_target_pairs={{0,8},{8,16},{16,24},{24,0},{1,9},{9,17},{17,25},{25,1},{2,10},{10... | collective-permute-start | bytes 776 | tf_op jit(solution)/shard_map/ppermute | solution.py:48
  187.4 3.6 %collective-permute-start.28 = (f32[1,256]{1,0:T(1,128)S(1)}, f32[1,256]{1,0:T(1,128)S(1)}, u32[]{:S(2)}, u32[]{:S(2)}) collective-permute-start(f32[1,256]{1,0:T(1,128)S(1)} %get-tuple-element.364), channel_id=1, source_target_pairs={{0,8},{8,0},{16,24},{24,16},{1,9},{9,1},{17,25},{25,17},{2,10},{10... | collective-permute-start | bytes 3080 | tf_op jit(solution)/shard_map/ppermute | solution.py:26
  193.9 4.2 %collective-permute-start.26 = (f32[64,1]{1,0:T(8,128)S(1)}, f32[64,1]{1,0:T(8,128)S(1)}, u32[]{:S(2)}, u32[]{:S(2)}) collective-permute-start(f32[64,1]{1,0:T(8,128)S(1)} %slice.599), channel_id=1, source_target_pairs={{0,24},{8,0},{16,8},{24,16},{1,25},{9,1},{17,9},{25,17},{2,26},{10... | collective-permute-start | bytes 776 | tf_op jit(solution)/shard_map/ppermute | solution.py:48
  198.2 6.9 %collective-permute-start.31 = (f32[1,256]{1,0:T(1,128)S(1)}, f32[1,256]{1,0:T(1,128)S(1)}, u32[]{:S(2)}, u32[]{:S(2)}) collective-permute-start(f32[1,256]{1,0:T(1,128)S(1)} %slice.605), channel_id=1, source_target_pairs={{0,1},{1,2},{2,3},{3,4},{4,5},{5,6},{6,7},{8,9},{9,10},{10,11},{11... | collective-permute-start | bytes 3080 | tf_op jit(solution)/shard_map/ppermute | solution.py:54
  200.3 4.8 %collective-permute-start.27 = (f32[64,1]{1,0:T(8,128)S(1)}, f32[64,1]{1,0:T(8,128)S(1)}, u32[]{:S(2)}, u32[]{:S(2)}) collective-permute-start(f32[64,1]{1,0:T(8,128)S(1)} %slice.600), channel_id=1, source_target_pairs={{0,8},{8,16},{16,24},{24,0},{1,9},{9,17},{17,25},{25,1},{2,10},{10... | collective-permute-start | bytes 776 | tf_op jit(solution)/shard_map/ppermute | solution.py:48
  205.2 3.6 %collective-permute-start.34 = (f32[1,256]{1,0:T(1,128)S(1)}, f32[1,256]{1,0:T(1,128)S(1)}, u32[]{:S(2)}, u32[]{:S(2)}) collective-permute-start(f32[1,256]{1,0:T(1,128)S(1)} %get-tuple-element.360), channel_id=1, source_target_pairs={{0,8},{8,0},{16,24},{24,16},{1,9},{9,1},{17,25},{25,17},{2,10},{10... | collective-permute-start | bytes 3080 | tf_op jit(solution)/shard_map/ppermute | solution.py:26
  210.8 4.2 %collective-permute-start.32 = (f32[64,1]{1,0:T(8,128)S(1)}, f32[64,1]{1,0:T(8,128)S(1)}, u32[]{:S(2)}, u32[]{:S(2)}) collective-permute-start(f32[64,1]{1,0:T(8,128)S(1)} %slice.608), channel_id=1, source_target_pairs={{0,24},{8,0},{16,8},{24,16},{1,25},{9,1},{17,9},{25,17},{2,26},{10... | collective-permute-start | bytes 776 | tf_op jit(solution)/shard_map/ppermute | solution.py:48
  215.0 7.2 %collective-permute-start.37 = (f32[1,256]{1,0:T(1,128)S(1)}, f32[1,256]{1,0:T(1,128)S(1)}, u32[]{:S(2)}, u32[]{:S(2)}) collective-permute-start(f32[1,256]{1,0:T(1,128)S(1)} %slice.614), channel_id=1, source_target_pairs={{0,1},{1,2},{2,3},{3,4},{4,5},{5,6},{6,7},{8,9},{9,10},{10,11},{11... | collective-permute-start | bytes 3080 | tf_op jit(solution)/shard_map/ppermute | solution.py:54
  217.1 5.1 %collective-permute-start.33 = (f32[64,1]{1,0:T(8,128)S(1)}, f32[64,1]{1,0:T(8,128)S(1)}, u32[]{:S(2)}, u32[]{:S(2)}) collective-permute-start(f32[64,1]{1,0:T(8,128)S(1)} %slice.609), channel_id=1, source_target_pairs={{0,8},{8,16},{16,24},{24,0},{1,9},{9,17},{17,25},{25,1},{2,10},{10... | collective-permute-start | bytes 776 | tf_op jit(solution)/shard_map/ppermute | solution.py:48
  222.3 3.6 %collective-permute-start.40 = (f32[1,256]{1,0:T(1,128)S(1)}, f32[1,256]{1,0:T(1,128)S(1)}, u32[]{:S(2)}, u32[]{:S(2)}) collective-permute-start(f32[1,256]{1,0:T(1,128)S(1)} %get-tuple-element.356), channel_id=1, source_target_pairs={{0,8},{8,0},{16,24},{24,16},{1,9},{9,1},{17,25},{25,17},{2,10},{10... | collective-permute-start | bytes 3080 | tf_op jit(solution)/shard_map/ppermute | solution.py:26
  228.6 4.2 %collective-permute-start.38 = (f32[64,1]{1,0:T(8,128)S(1)}, f32[64,1]{1,0:T(8,128)S(1)}, u32[]{:S(2)}, u32[]{:S(2)}) collective-permute-start(f32[64,1]{1,0:T(8,128)S(1)} %slice.617), channel_id=1, source_target_pairs={{0,24},{8,0},{16,8},{24,16},{1,25},{9,1},{17,9},{25,17},{2,26},{10... | collective-permute-start | bytes 776 | tf_op jit(solution)/shard_map/ppermute | solution.py:48
  232.9 7.3 %collective-permute-start.43 = (f32[1,256]{1,0:T(1,128)S(1)}, f32[1,256]{1,0:T(1,128)S(1)}, u32[]{:S(2)}, u32[]{:S(2)}) collective-permute-start(f32[1,256]{1,0:T(1,128)S(1)} %slice.623), channel_id=1, source_target_pairs={{0,1},{1,2},{2,3},{3,4},{4,5},{5,6},{6,7},{8,9},{9,10},{10,11},{11... | collective-permute-start | bytes 3080 | tf_op jit(solution)/shard_map/ppermute | solution.py:54
  235.0 5.2 %collective-permute-start.39 = (f32[64,1]{1,0:T(8,128)S(1)}, f32[64,1]{1,0:T(8,128)S(1)}, u32[]{:S(2)}, u32[]{:S(2)}) collective-permute-start(f32[64,1]{1,0:T(8,128)S(1)} %slice.618), channel_id=1, source_target_pairs={{0,8},{8,16},{16,24},{24,0},{1,9},{9,17},{17,25},{25,1},{2,10},{10... | collective-permute-start | bytes 776 | tf_op jit(solution)/shard_map/ppermute | solution.py:48
  240.2 3.6 %collective-permute-start.46 = (f32[1,256]{1,0:T(1,128)S(1)}, f32[1,256]{1,0:T(1,128)S(1)}, u32[]{:S(2)}, u32[]{:S(2)}) collective-permute-start(f32[1,256]{1,0:T(1,128)S(1)} %get-tuple-element.352), channel_id=1, source_target_pairs={{0,8},{8,0},{16,24},{24,16},{1,9},{9,1},{17,25},{25,17},{2,10},{10... | collective-permute-start | bytes 3080 | tf_op jit(solution)/shard_map/ppermute | solution.py:26
  246.0 4.2 %collective-permute-start.44 = (f32[64,1]{1,0:T(8,128)S(1)}, f32[64,1]{1,0:T(8,128)S(1)}, u32[]{:S(2)}, u32[]{:S(2)}) collective-permute-start(f32[64,1]{1,0:T(8,128)S(1)} %slice.626), channel_id=1, source_target_pairs={{0,24},{8,0},{16,8},{24,16},{1,25},{9,1},{17,9},{25,17},{2,26},{10... | collective-permute-start | bytes 776 | tf_op jit(solution)/shard_map/ppermute | solution.py:48
  250.3 7.3 %collective-permute-start.49 = (f32[1,256]{1,0:T(1,128)S(1)}, f32[1,256]{1,0:T(1,128)S(1)}, u32[]{:S(2)}, u32[]{:S(2)}) collective-permute-start(f32[1,256]{1,0:T(1,128)S(1)} %slice.632), channel_id=1, source_target_pairs={{0,1},{1,2},{2,3},{3,4},{4,5},{5,6},{6,7},{8,9},{9,10},{10,11},{11... | collective-permute-start | bytes 3080 | tf_op jit(solution)/shard_map/ppermute | solution.py:54
  252.4 5.2 %collective-permute-start.45 = (f32[64,1]{1,0:T(8,128)S(1)}, f32[64,1]{1,0:T(8,128)S(1)}, u32[]{:S(2)}, u32[]{:S(2)}) collective-permute-start(f32[64,1]{1,0:T(8,128)S(1)} %slice.627), channel_id=1, source_target_pairs={{0,8},{8,16},{16,24},{24,0},{1,9},{9,17},{17,25},{25,1},{2,10},{10... | collective-permute-start | bytes 776 | tf_op jit(solution)/shard_map/ppermute | solution.py:48
  257.7 3.6 %collective-permute-start.52 = (f32[1,256]{1,0:T(1,128)S(1)}, f32[1,256]{1,0:T(1,128)S(1)}, u32[]{:S(2)}, u32[]{:S(2)}) collective-permute-start(f32[1,256]{1,0:T(1,128)S(1)} %get-tuple-element.348), channel_id=1, source_target_pairs={{0,8},{8,0},{16,24},{24,16},{1,9},{9,1},{17,25},{25,17},{2,10},{10... | collective-permute-start | bytes 3080 | tf_op jit(solution)/shard_map/ppermute | solution.py:26
  264.0 4.2 %collective-permute-start.50 = (f32[64,1]{1,0:T(8,128)S(1)}, f32[64,1]{1,0:T(8,128)S(1)}, u32[]{:S(2)}, u32[]{:S(2)}) collective-permute-start(f32[64,1]{1,0:T(8,128)S(1)} %slice.635), channel_id=1, source_target_pairs={{0,24},{8,0},{16,8},{24,16},{1,25},{9,1},{17,9},{25,17},{2,26},{10... | collective-permute-start | bytes 776 | tf_op jit(solution)/shard_map/ppermute | solution.py:48
  268.2 7.4 %collective-permute-start.55 = (f32[1,256]{1,0:T(1,128)S(1)}, f32[1,256]{1,0:T(1,128)S(1)}, u32[]{:S(2)}, u32[]{:S(2)}) collective-permute-start(f32[1,256]{1,0:T(1,128)S(1)} %slice.641), channel_id=1, source_target_pairs={{0,1},{1,2},{2,3},{3,4},{4,5},{5,6},{6,7},{8,9},{9,10},{10,11},{11... | collective-permute-start | bytes 3080 | tf_op jit(solution)/shard_map/ppermute | solution.py:54
  270.5 5.2 %collective-permute-start.51 = (f32[64,1]{1,0:T(8,128)S(1)}, f32[64,1]{1,0:T(8,128)S(1)}, u32[]{:S(2)}, u32[]{:S(2)}) collective-permute-start(f32[64,1]{1,0:T(8,128)S(1)} %slice.636), channel_id=1, source_target_pairs={{0,8},{8,16},{16,24},{24,0},{1,9},{9,17},{17,25},{25,1},{2,10},{10... | collective-permute-start | bytes 776 | tf_op jit(solution)/shard_map/ppermute | solution.py:48
  275.8 3.6 %collective-permute-start.58 = (f32[1,256]{1,0:T(1,128)S(1)}, f32[1,256]{1,0:T(1,128)S(1)}, u32[]{:S(2)}, u32[]{:S(2)}) collective-permute-start(f32[1,256]{1,0:T(1,128)S(1)} %get-tuple-element.344), channel_id=1, source_target_pairs={{0,8},{8,0},{16,24},{24,16},{1,9},{9,1},{17,25},{25,17},{2,10},{10... | collective-permute-start | bytes 3080 | tf_op jit(solution)/shard_map/ppermute | solution.py:26
  281.5 4.2 %collective-permute-start.56 = (f32[64,1]{1,0:T(8,128)S(1)}, f32[64,1]{1,0:T(8,128)S(1)}, u32[]{:S(2)}, u32[]{:S(2)}) collective-permute-start(f32[64,1]{1,0:T(8,128)S(1)} %slice.644), channel_id=1, source_target_pairs={{0,24},{8,0},{16,8},{24,16},{1,25},{9,1},{17,9},{25,17},{2,26},{10... | collective-permute-start | bytes 776 | tf_op jit(solution)/shard_map/ppermute | solution.py:48
  285.8 7.3 %collective-permute-start.61 = (f32[1,256]{1,0:T(1,128)S(1)}, f32[1,256]{1,0:T(1,128)S(1)}, u32[]{:S(2)}, u32[]{:S(2)}) collective-permute-start(f32[1,256]{1,0:T(1,128)S(1)} %slice.650), channel_id=1, source_target_pairs={{0,1},{1,2},{2,3},{3,4},{4,5},{5,6},{6,7},{8,9},{9,10},{10,11},{11... | collective-permute-start | bytes 3080 | tf_op jit(solution)/shard_map/ppermute | solution.py:54
  287.9 5.2 %collective-permute-start.57 = (f32[64,1]{1,0:T(8,128)S(1)}, f32[64,1]{1,0:T(8,128)S(1)}, u32[]{:S(2)}, u32[]{:S(2)}) collective-permute-start(f32[64,1]{1,0:T(8,128)S(1)} %slice.645), channel_id=1, source_target_pairs={{0,8},{8,16},{16,24},{24,0},{1,9},{9,17},{17,25},{25,1},{2,10},{10... | collective-permute-start | bytes 776 | tf_op jit(solution)/shard_map/ppermute | solution.py:48
  293.2 3.6 %collective-permute-start.63 = (f32[1,256]{1,0:T(1,128)S(1)}, f32[1,256]{1,0:T(1,128)S(1)}, u32[]{:S(2)}, u32[]{:S(2)}) collective-permute-start(f32[1,256]{1,0:T(1,128)S(1)} %get-tuple-element.340), channel_id=1, source_target_pairs={{0,8},{8,0},{16,24},{24,16},{1,9},{9,1},{17,25},{25,17},{2,10},{10... | collective-permute-start | bytes 3080 | tf_op jit(solution)/shard_map/ppermute | solution.py:26
  293.3 7.3 %collective-permute-start.65 = (f32[1,256]{1,0:T(1,128)S(1)}, f32[1,256]{1,0:T(1,128)S(1)}, u32[]{:S(2)}, u32[]{:S(2)}) collective-permute-start(f32[1,256]{1,0:T(1,128)S(1)} %get-tuple-element.339), channel_id=1, source_target_pairs={{1,0},{2,1},{3,2},{4,3},{5,4},{6,5},{7,6},{9,8},{10,9},{11,10},{12... | collective-permute-start | bytes 3080 | tf_op jit(solution)/shard_map/ppermute | solution.py:54
  299.9 4.0 %collective-permute-start.62 = (f32[64,1]{1,0:T(8,128)S(1)}, f32[64,1]{1,0:T(8,128)S(1)}, u32[]{:S(2)}, u32[]{:S(2)}) collective-permute-start(f32[64,1]{1,0:T(8,128)S(1)} %slice.653), channel_id=1, source_target_pairs={{0,24},{8,0},{16,8},{24,16},{1,25},{9,1},{17,9},{25,17},{2,26},{10... | collective-permute-start | bytes 776 | tf_op jit(solution)/shard_map/ppermute | solution.py:48
  (32 other events, 282.7 us)
where the time goes:
time: 319 us; the launch traced here: 317 us
  waiting for transfers between devices  106 us (33%)
  other arithmetic  90.2 us (28%)
  starting transfers between devices  71.6 us (22%)
  local copies, waits for them, and re-layouts  35.7 us (11%)
  blocking collectives  11.7 us (4%)
    ppermute x20, waiting for transfers between devices, passed_along(): return lax.ppermute(value, axis, pairs)  60.3 us
    ppermute x22, waiting for transfers between devices, partner(): return lax.ppermute(block, axis, route)  38.5 us
    ppermute x20, starting transfers between devices, shifted(): return lax.ppermute(array, axis, pairs)  31.7 us
    dynamic_update_slice x30, other arithmetic, body(): lax.scan(per_level, start, (state_ext[0], state_ext[1], state_ext[2], sta...  26 us
    add x10, other arithmetic, level_core(): pressure = above_sum + 0.5 * layer_weight  16.6 us
    ppermute x22, starting transfers between devices, partner(): return lax.ppermute(block, axis, route)  16 us
    ppermute x20, starting transfers between devices, passed_along(): return lax.ppermute(value, axis, pairs)  14.2 us
    add x10, other arithmetic, level_core(): col_depth = col_depth + wet_cells * thick_k  13.5 us
  transfers between devices with their start and end apart: 66, of which 43 were waited for; matrix products, arithmetic and copies ran while one was open for 36% of the time, Pallas kernels for 0%

commit v1 on v0

v1 whole, which is shorter than its diff:
```python
import functools
import math

import jax
import jax.numpy as jnp
from jax import lax
from jax.experimental import pallas as pl
from jax.experimental.pallas import tpu as pltpu
from jax.sharding import PartitionSpec as P

NSUB = 10
RIM = 16
CH = 16
LANES = 128
F32 = jnp.float32
MESH = pl.DeviceIdType.MESH


def iota(shape, dim):
    return lax.broadcasted_iota(jnp.int32, shape, dim)


def exact_dot(a, b):
    return jnp.dot(a, b, precision=lax.Precision.HIGHEST, preferred_element_type=F32)


def anti(size):
    return (iota((size, size), 0) + iota((size, size), 1) == size - 1).astype(F32)


def anti_blocks(size, block):
    a, b = iota((size, size), 0), iota((size, size), 1)
    same = (a // block) == (b // block)
    return (same & (a % block + b % block == block - 1)).astype(F32)


def remote(src, dst, send, recv, where):
    return pltpu.make_async_remote_copy(
        src_ref=src, dst_ref=dst, send_sem=send, recv_sem=recv, device_id=where, device_id_type=MESH
    )


def kernel(
    nlat, nlon, K, R, C,
    st_hbm, s_hbm, u_hbm, v_hbm, mask_hbm, lev_hbm,
    ns, os_ref, ou_ref, ov_ref, op_ref,
    ts, uv, pr, ml, w, le, ln, fw0, fs0,
    pcw, pce, re, rw, pkn, pks, rn, rs, fold1, fold4, foldf,
    c2w, c2e, r2e, r2w, ae, an, dd, gg, tot, totr,
    lsem, ssem, rsem, tssem, trsem,
):
    lat, lon = lax.axis_index("lat"), lax.axis_index("lon")
    east, west = lax.rem(lon + 1, nlon), lax.rem(lon + nlon - 1, nlon)
    up, down = lax.rem(lat + 1, nlat), lax.rem(lat + nlat - 1, nlat)
    is_top, is_low = lat == nlat - 1, lat == 0
    not_top, not_low = lat < nlat - 1, lat > 0
    turned = nlon - 1 - lon
    W = C + LANES
    c0, c1 = RIM, RIM + R
    last = C - LANES

    barrier = pltpu.get_barrier_semaphore()
    for d in range(1, nlon):
        pl.semaphore_signal(
            barrier, inc=1, device_id={"lon": lax.rem(lon + d, nlon)}, device_id_type=MESH
        )
    for d in range(1, nlat):
        pl.semaphore_signal(
            barrier, inc=1, device_id={"lat": lax.rem(lat + d, nlat)}, device_id_type=MESH
        )

    loads = [
        pltpu.make_async_copy(mask_hbm, ml.at[0], lsem.at[0]),
        pltpu.make_async_copy(lev_hbm, ml.at[1], lsem.at[1]),
        pltpu.make_async_copy(st_hbm.at[0:2], ts.at[:, :, 0:R, :], lsem.at[2]),
        pltpu.make_async_copy(st_hbm.at[2:4], uv, lsem.at[3]),
        pltpu.make_async_copy(s_hbm, w.at[0, c0:c1, 0:C], lsem.at[4]),
        pltpu.make_async_copy(u_hbm, w.at[1, c0:c1, 0:C], lsem.at[5]),
        pltpu.make_async_copy(v_hbm, w.at[2, c0:c1, 0:C], lsem.at[6]),
    ]
    for load in loads:
        load.start()

    col_w = remote(pcw, re, ssem.at[0], rsem.at[0], {"lon": west})
    col_e = remote(pce, rw, ssem.at[1], rsem.at[1], {"lon": east})
    row_n = remote(pkn, rs, ssem.at[2], rsem.at[2], {"lat": up})
    row_s = remote(pks, rn, ssem.at[3], rsem.at[3], {"lat": down})
    row_f = remote(fold1, rn, ssem.at[2], rsem.at[3], {"lon": turned})
    hi, lo = pl.ds(c1 - RIM, RIM), pl.ds(c0, RIM)
    above, below = pl.ds(c1, RIM), pl.ds(0, RIM)
    cols = pl.ds(0, C)
    four, two = pl.ds(0, 4), pl.ds(4, 2)
    wid_n = remote(w.at[four, hi, cols], w.at[four, below, cols], ssem.at[4], rsem.at[4], {"lat": up})
    wid_s = remote(w.at[four, lo, cols], w.at[four, above, cols], ssem.at[5], rsem.at[5], {"lat": down})
    wid_f = remote(fold4, w.at[four, above, cols], ssem.at[4], rsem.at[5], {"lon": turned})
    frc_n = remote(w.at[two, hi, cols], w.at[two, below, cols], ssem.at[6], rsem.at[6], {"lat": up})
    frc_s = remote(w.at[two, lo, cols], w.at[two, above, cols], ssem.at[7], rsem.at[7], {"lat": down})
    frc_f = remote(foldf, w.at[two, above, cols], ssem.at[6], rsem.at[7], {"lon": turned})
    far_w = remote(c2w, r2e, ssem.at[8], rsem.at[8], {"lon": west})
    far_e = remote(c2e, r2w, ssem.at[9], rsem.at[9], {"lon": east})

    @pl.when(is_low)
    def _():
        w[:, 0:RIM, 0:C] = jnp.zeros((6, RIM, C), F32)
        rs[...] = jnp.zeros(rs.shape, F32)

    dd[...] = jnp.zeros(dd.shape, F32)
    gg[...] = jnp.zeros(gg.shape, F32)

    lane = iota((CH, LANES), 1)
    lane_c = iota((CH, C), 1)
    row_c = iota((CH, C), 0)
    chunks = range(0, R, CH)
    loads[0].wait()
    loads[1].wait()
    for r in chunks:
        level = (ml[0, r : r + CH, :] * ml[1, r : r + CH, :]).astype(F32)
        w[3, c0 + r : c0 + r + CH, 0:C] = level
        l0, l1 = level[:, :LANES], level[:, last:]
        pcw[r : r + CH, :] = jnp.where(lane == 3 * K, pltpu.roll(l0, 3 * K, 1), 0.0)
        pce[r : r + CH, :] = jnp.where(lane == 3 * K, pltpu.roll(l1, 3 * K + 1, 1), 0.0)
    loads[2].wait()
    loads[3].wait()
    per = 2.0 / (K * (K + 1))

    def pressure_level(k, sums):
        kf = k.astype(F32)
        thick = (kf + 1.0) * per
        out = []
        for i, r in enumerate(chunks):
            rr = slice(r, r + CH)
            t, s = ts[0, k, rr, :], ts[1, k, rr, :]
            level = w[3, c0 + r : c0 + r + CH, 0:C]
            weight = jnp.where(kf < level, 0.8 * s - 0.3 * t - 0.04 * t * t, 0.0) * thick
            press = sums[i] + 0.5 * weight
            out.append(sums[i] + weight)
            pr[k, rr, :] = press
            u1 = uv[0, k, rr, last:]
            t0, s0, p0 = t[:, :LANES], s[:, :LANES], press[:, :LANES]
            t1, s1 = t[:, last:], s[:, last:]
            a = pcw[rr, :]
            a = jnp.where(lane == k, pltpu.roll(t0, k, 1), a)
            a = jnp.where(lane == K + k, pltpu.roll(s0, K + k, 1), a)
            a = jnp.where(lane == 2 * K + k, pltpu.roll(p0, 2 * K + k, 1), a)
            pcw[rr, :] = a
            b = pce[rr, :]
            b = jnp.where(lane == k, pltpu.roll(t1, k + 1, 1), b)
            b = jnp.where(lane == K + k, pltpu.roll(s1, K + k + 1, 1), b)
            b = jnp.where(lane == 2 * K + k, pltpu.roll(u1, 2 * K + k + 1, 1), b)
            pce[rr, :] = b
        return tuple(out)

    lax.fori_loop(0, K, pressure_level, tuple(jnp.zeros((CH, C), F32) for _ in chunks))
    for k in range(K):
        pkn[k : k + 1, :] = ts[0, k, R - 1 : R, :]
        pkn[K + k : K + k + 1, :] = ts[1, k, R - 1 : R, :]
        pkn[2 * K + k : 2 * K + k + 1, :] = uv[1, k, R - 1 : R, :]
        pks[k : k + 1, :] = ts[0, k, 0:1, :]
        pks[K + k : K + k + 1, :] = ts[1, k, 0:1, :]
        pks[2 * K + k : 2 * K + k + 1, :] = pr[k, 0:1, :]
    pkn[3 * K : 3 * K + 1, :] = w[3, c1 - 1 : c1, 0:C]
    pks[3 * K : 3 * K + 1, :] = w[3, c0 : c0 + 1, 0:C]

    pl.semaphore_wait(barrier, nlat + nlon - 2)

    @pl.when(is_top)
    def _():
        for k in range(K):
            fold1[k : k + 1, :] = ts[0, k, R - 1 : R, :]
            fold1[K + k : K + k + 1, :] = ts[1, k, R - 1 : R, :]
            fold1[2 * K + k : 2 * K + k + 1, :] = pr[k, R - 1 : R, :]
        fold1[3 * K : 3 * K + 1, :] = w[3, c1 - 1 : c1, 0:C]
        fold1[3 * K + 1 :, :] = jnp.zeros((fold1.shape[0] - 3 * K - 1, C), F32)
        fold1[...] = exact_dot(fold1[...], anti(C))
        row_f.start()

    col_w.start()
    col_e.start()

    @pl.when(not_top)
    def _():
        row_n.start()

    @pl.when(not_low)
    def _():
        row_s.start()

    for load in loads[4:]:
        load.wait()

    @pl.when(not_top)
    def _():
        wid_n.start()

    @pl.when(is_top)
    def _():
        rows4 = jnp.concatenate([w[f, c1 - RIM : c1, 0:C] for f in range(4)], axis=0)
        flipped = exact_dot(exact_dot(anti_blocks(4 * RIM, RIM), rows4), anti(C))
        for f in range(4):
            fold4[f] = flipped[f * RIM : (f + 1) * RIM]
        wid_f.start()

    @pl.when(not_low)
    def _():
        wid_s.start()

    col_w.wait_recv()
    row_s.wait_recv()
    for k in range(K):
        ts[0, k, R : R + 1, :] = rn[k : k + 1, :]
        ts[1, k, R : R + 1, :] = rn[K + k : K + k + 1, :]
        pr[k, R : R + 1, :] = rn[2 * K + k : 2 * K + k + 1, :]

    def eastward(centre, rim, shift):
        rolled = pltpu.roll(centre, C - 1, 1)
        h = pltpu.roll(rim, shift, 1)
        edge = jnp.where(lane == LANES - 1, h, rolled[:, last:])
        return jnp.concatenate([rolled[:, :last], edge], axis=1)

    for r in chunks:
        level = w[3, c0 + r : c0 + r + CH, 0:C]
        le[r : r + CH, :] = jnp.minimum(
            level, eastward(level, re[r : r + CH, :], LANES - 1 - 3 * K)
        )
        if r + CH < R:
            north = w[3, c0 + r + 1 : c0 + r + CH + 1, 0:C]
        else:
            north = jnp.where(
                row_c == CH - 1, rn[3 * K : 3 * K + 1, :], pltpu.roll(level, CH - 1, 0)
            )
        ln[r : r + CH, :] = jnp.minimum(level, north)

    for r in chunks:
        rr = slice(r, r + CH)
        le_r, ln_r, rim = le[rr, :], ln[rr, :], re[rr, :]

        def force_level(k, sums):
            fx, fy = sums
            kf = k.astype(F32)
            thick = (kf + 1.0) * per
            press = pr[k, rr, :]
            p_e = eastward(press, rim, LANES - 1 - 2 * K - k)
            p_n = pr[k, r + 1 : r + CH + 1, :]
            open_e, open_n = kf < le_r, kf < ln_r
            gx = jnp.where(open_e, p_e - press, 0.0)
            gy = jnp.where(open_n, p_n - press, 0.0)
            ns[2, k, rr, :] = jnp.where(open_e, uv[0, k, rr, :] - 0.2 * gx, 0.0)
            ns[3, k, rr, :] = jnp.where(open_n, uv[1, k, rr, :] - 0.2 * gy, 0.0)
            return fx + gx * thick, fy + gy * thick

        zero = jnp.zeros((CH, C), F32)
        fx, fy = lax.fori_loop(0, K, force_level, (zero, zero))
        w[4, c0 + r : c0 + r + CH, 0:C] = 0.1 * fx
        w[5, c0 + r : c0 + r + CH, 0:C] = 0.1 * fy

    @pl.when(not_top)
    def _():
        frc_n.start()

    @pl.when(is_top)
    def _():
        rows2 = jnp.concatenate([w[f, c1 - RIM : c1, 0:C] for f in (4, 5)], axis=0)
        flipped = exact_dot(exact_dot(anti_blocks(2 * RIM, RIM), rows2), anti(C))
        foldf[0] = flipped[:RIM]
        foldf[1] = flipped[RIM:]
        frc_f.start()

    @pl.when(not_low)
    def _():
        frc_s.start()

    col_e.wait_recv()

    @pl.when(not_low)
    def _():
        row_n.wait_recv()

    lane_f = jnp.where(lane < K, lane, lane - K).astype(F32)
    for r in chunks:
        rr = slice(r, r + CH)
        a, b = rw[rr, :], pcw[rr, :]
        u = jnp.where(lane < K, pltpu.roll(a, LANES - 2 * K, 1), pltpu.roll(a, LANES - K, 1))
        shallow = jnp.minimum(a[:, 3 * K : 3 * K + 1], b[:, 3 * K : 3 * K + 1])
        flux = (jnp.maximum(u, 0.0) + 0.1) * a + (jnp.minimum(u, 0.0) - 0.1) * b
        fw0[rr, :] = jnp.where(lane_f < shallow, flux, 0.0)
    row_k = iota((K, C), 0).astype(F32)
    shallow = jnp.minimum(rs[3 * K : 3 * K + 1, :], pks[3 * K : 3 * K + 1, :])
    v_rim = rs[2 * K : 3 * K, :]
    vp, vm = jnp.maximum(v_rim, 0.0) + 0.1, jnp.minimum(v_rim, 0.0) - 0.1
    for q in range(2):
        flux = vp * rs[q * K : (q + 1) * K, :] + vm * pks[q * K : (q + 1) * K, :]
        flux = jnp.where(row_k < shallow, flux, 0.0)
        for k in range(K):
            fs0[q, k] = flux[k : k + 1, :]

    def tracer_level(k, carry):
        kf = k.astype(F32)
        south_row = [fs0[q, k] for q in range(2)]
        for r in chunks:
            rr = slice(r, r + CH)
            u, v = uv[0, k, rr, :], uv[1, k, rr, :]
            u_p, u_m = jnp.maximum(u, 0.0) + 0.1, jnp.minimum(u, 0.0) - 0.1
            v_p, v_m = jnp.maximum(v, 0.0) + 0.1, jnp.minimum(v, 0.0) - 0.1
            wet = kf < w[3, c0 + r : c0 + r + CH, 0:C]
            wet_e, wet_n = kf < le[rr, :], kf < ln[rr, :]
            rim_e, rim_w = re[rr, :], fw0[rr, :]
            for q in range(2):
                c = ts[q, k, rr, :]
                fe = jnp.where(
                    wet_e, u_p * c + u_m * eastward(c, rim_e, LANES - 1 - q * K - k), 0.0
                )
                fn = jnp.where(wet_n, v_p * c + v_m * ts[q, k, r + 1 : r + CH + 1, :], 0.0)
                h = pltpu.roll(rim_w, LANES - q * K - k if q else lax.rem(LANES - k, LANES), 1)
                rolled = pltpu.roll(fe, 1, 1)
                fw = jnp.concatenate(
                    [jnp.where(lane == 0, h, rolled[:, :LANES]), rolled[:, LANES:]], axis=1
                )
                fs = jnp.where(row_c == 0, south_row[q], pltpu.roll(fn, 1, 0))
                south_row[q] = fn[CH - 1 : CH, :]
                ns[q, k, rr, :] = jnp.where(wet, c + 0.2 * (fw - fe + fs - fn), 0.0)
        return carry

    first, second = (4 * K) // 10, (8 * K) // 10
    lax.fori_loop(0, first, tracer_level, 0)

    wid_s.wait_recv()
    frc_s.wait_recv()

    @pl.when(not_low)
    def _():
        wid_n.wait_recv()
        frc_n.wait_recv()

    wide_rows = range(0, R + 2 * RIM, CH)
    for r in wide_rows:
        a = jnp.zeros((CH, LANES), F32)
        b = jnp.zeros((CH, LANES), F32)
        for f in range(6):
            mine = (lane >= f * RIM) & (lane < (f + 1) * RIM)
            x0 = w[f, r : r + CH, 0:LANES]
            x1 = w[f, r : r + CH, last:C]
            a = jnp.where(mine, pltpu.roll(x0, f * RIM, 1) if f else x0, a)
            b = jnp.where(mine, pltpu.roll(x1, (RIM + f * RIM) % LANES, 1), b)
        c2w[r : r + CH, :] = a
        c2e[r : r + CH, :] = b
    far_w.start()
    far_e.start()
    lax.fori_loop(first, second, tracer_level, 0)
    far_w.wait_recv()
    far_e.wait_recv()
    for r in wide_rows:
        a, b = r2e[r : r + CH, :], r2w[r : r + CH, :]
        for f in range(6):
            x = pltpu.roll(a, LANES - f * RIM, 1) if f else a
            y = pltpu.roll(b, (LANES - RIM - f * RIM) % LANES, 1)
            w[f, r : r + CH, C:W] = jnp.where(
                lane < RIM, x, jnp.where(lane >= LANES - RIM, y, 0.0)
            )

    @pl.when(not_top)
    def _():
        row_n.wait_send()
        wid_n.wait_send()
        frc_n.wait_send()

    @pl.when(not_low)
    def _():
        row_s.wait_send()
        wid_s.wait_send()
        frc_s.wait_send()

    lane_w = iota((CH, W), 1)
    row_w = iota((CH, W), 0)

    @pl.when(is_top)
    def _():
        row_f.wait_send()
        wid_f.wait_send()
        frc_f.wait_send()
        fold = slice(c1, c1 + RIM)
        for f in (1, 4):
            w[f, fold, :] = -pltpu.roll(w[f, fold, :], W - 1, 1)
        for f, where in ((2, dd), (5, gg)):
            x = w[f, fold, :]
            where[...] = jnp.where(row_w == 0, w[f, c1 - 1 : c1, :] + x, 0.0)
            w[f, fold, :] = -pltpu.roll(x, RIM - 1, 0)

    def wide_depth(shallow):
        return (shallow * (shallow + 1.0)) * (0.8 / (K * (K + 1)))

    def shifted_rows(ref, f, r, by):
        low = r + by
        if low < 0 or low + CH > R + 2 * RIM:
            return pltpu.roll(ref[f, r : r + CH, :], (-by) % CH, 0)
        return ref[f, low : low + CH, :]

    def surface_step(first_step):
        for r in wide_rows:
            rr = slice(r, r + CH)
            u, v = w[1, rr, :], w[2, rr, :]
            div = u - pltpu.roll(u, 1, 1) + (v - shifted_rows(w, 2, r, -1))
            if r == c1:
                div = div + dd[...]
            new = w[0, rr, :] - 0.5 * div
            if first_step:
                new = jnp.where(w[3, rr, :] > 0.0, new, 0.0)
            w[0, rr, :] = new

    def transport_step(first_step):
        for r in wide_rows:
            rr = slice(r, r + CH)
            s, u, v = w[0, rr, :], w[1, rr, :], w[2, rr, :]
            if first_step:
                level = w[3, rr, :]
                shallow_e = jnp.minimum(level, pltpu.roll(level, W - 1, 1))
                shallow_n = jnp.minimum(level, shifted_rows(w, 3, r, 1))
                ae[rr, :] = wide_depth(shallow_e)
                an[rr, :] = wide_depth(shallow_n)
                u = jnp.where(shallow_e > 0.0, u, 0.0)
                v = jnp.where(shallow_n > 0.0, v, 0.0)
            w[1, rr, :] = u - ae[rr, :] * (pltpu.roll(s, W - 1, 1) - s) - w[4, rr, :]
            w[2, rr, :] = v - an[rr, :] * (shifted_rows(w, 0, r, 1) - s) - w[5, rr, :]

    surface_step(True)
    transport_step(True)
    dd[...] = jnp.where(an[c1 - 1 : c1, :] > 0.0, dd[...], 0.0) - gg[...]

    def substep(i, carry):
        surface_step(False)
        transport_step(False)
        dd[...] = dd[...] - gg[...]
        return carry

    lax.fori_loop(1, NSUB, substep, 0)

    low_tri = (iota((R, R), 0) >= iota((R, R), 1)).astype(F32)
    zonal = w[1, c0:c1, 0:C]
    op_ref[...] = exact_dot(low_tri, zonal)
    tot[...] = jnp.broadcast_to(op_ref[R - 1 : R, :], tot.shape)
    sends = []
    for d in range(1, nlat):
        sends.append(
            remote(
                tot, totr.at[d - 1], tssem.at[d - 1], trsem.at[d - 1],
                {"lat": lax.rem(lat + d, nlat)},
            )
        )
    for send in sends:
        send.start()
    lax.fori_loop(second, K, tracer_level, 0)
    os_ref[...] = w[0, c0:c1, 0:C]
    ou_ref[...] = zonal
    ov_ref[...] = w[2, c0:c1, 0:C]
    south = jnp.zeros((8, C), F32)
    for d in range(1, nlat):
        sends[d - 1].wait_recv()
        south = south + totr[d - 1] * (lat >= d).astype(F32)
    scale = -1.0 / math.sqrt(R * nlat)
    op_ref[...] = (op_ref[...] + south[0:1, :]) * scale
    for send in sends:
        send.wait_send()
    for copy in (col_w, col_e, far_w, far_e):
        copy.wait_send()


def body(ocean_state, surface_height, zonal_transport, meridional_transport, land_mask, levels):
    nlat, nlon = lax.axis_size("lat"), lax.axis_size("lon")
    _, K, R, C = ocean_state.shape
    wide = (R + 2 * RIM, C + LANES)
    plane = jax.ShapeDtypeStruct((R, C), F32)
    pack = -(-(3 * K + 1) // 8) * 8
    vm = lambda *shape: pltpu.VMEM(shape, F32)
    dma = lambda n: pltpu.SemaphoreType.DMA((n,))
    return pl.pallas_call(
        functools.partial(kernel, nlat, nlon, K, R, C),
        out_shape=(jax.ShapeDtypeStruct(ocean_state.shape, F32), plane, plane, plane, plane),
        in_specs=[pl.BlockSpec(memory_space=pltpu.HBM)] * 6,
        out_specs=(pl.BlockSpec(memory_space=pltpu.VMEM),) * 5,
        scratch_shapes=[
            vm(2, K, R + 8, C), vm(2, K, R, C), vm(K, R + 8, C),
            pltpu.VMEM((2, R, C), jnp.int32),
            vm(6, *wide), vm(R, C), vm(R, C), vm(R, LANES), vm(2, K, 1, C),
            vm(R, LANES), vm(R, LANES), vm(R, LANES), vm(R, LANES),
            vm(pack, C), vm(pack, C), vm(pack, C), vm(pack, C), vm(pack, C),
            vm(4, RIM, C), vm(2, RIM, C),
            vm(wide[0], LANES), vm(wide[0], LANES), vm(wide[0], LANES), vm(wide[0], LANES),
            vm(*wide), vm(*wide), vm(RIM, wide[1]), vm(RIM, wide[1]),
            vm(8, C), vm(nlat - 1, 8, C),
            dma(7), dma(10), dma(10), dma(nlat - 1), dma(nlat - 1),
        ],
        compiler_params=pltpu.CompilerParams(
            collective_id=0, has_side_effects=True, vmem_limit_bytes=40 * 1024 * 1024
        ),
        cost_estimate=pl.CostEstimate(
            flops=40_000_000, bytes_accessed=2 * ocean_state.size * 4, transcendentals=0
        ),
    )(ocean_state, surface_height, zonal_transport, meridional_transport, land_mask, levels)


def solution(mesh):
    cells = P("lat", "lon")
    full = P(None, None, "lat", "lon")
    return jax.shard_map(
        body,
        mesh=mesh,
        in_specs=(full, cells, cells, cells, cells, cells),
        out_specs=(full, cells, cells, cells, cells),
        check_vma=False,
    )
```

time: 319 us -> 36.7 us (0.12)
  waiting for transfers between devices: 106 us -> 0 us
  other arithmetic: 90.2 us -> 0 us
  starting transfers between devices: 71.6 us -> 0 us
  Pallas kernels: 0 us -> 25.8 us
  local copies, waits for them, and re-layouts: 35.7 us -> 9.94 us
  blocking collectives: 11.7 us -> 0 us
    ppermute x66 -> x0, waiting for transfers between devices: 106 us -> none  [the longest x20 60.3 us: passed_along(): return lax.ppermute(value, axis, pairs)]
    ppermute x66 -> x0, starting transfers between devices: 71.6 us -> none  [the longest x20 31.7 us: shifted(): return lax.ppermute(array, axis, pairs)]
    add x40 -> x0, other arithmetic: 45 us -> none  [the longest x10 16.6 us: level_core(): pressure = above_sum + 0.5 * layer_weight]
    dynamic_update_slice x30 -> x0, other arithmetic: 26 us -> none  [body(): lax.scan(per_level, start, (state_ext[0], state_ext[1], state_ext[2], sta...]
    pallas_call x0 -> x1, Pallas kernels: none -> 25.8 us  [body(): pl.pallas_call(functools.partial(kernel, nlat, nlon, K, R, C), out_shape=...]
    dynamic_slice x27 -> x0, local copies, waits for them, and re-layouts: 11.7 us -> none  [the longest x20 11.7 us: body(): lax.scan(per_level, start, (state_ext[0], state_ext[1], state_ext[2], sta...]
    all_gather x1 -> x0, blocking collectives: 11.7 us -> none  [entering(): pieces = lax.all_gather(value, axis)]
    unnamed x31 -> x17, local copies, waits for them, and re-layouts: 0.07 us -> 9.94 us
  transfers between devices with their start and end apart: 66 -> 0, of which waited for: 43 -> 0; matrix products, arithmetic and copies ran while one was open for 36% -> 0% of each run, Pallas kernels for 0% -> 0%
where the time goes in v1:
time: 36.7 us; the launch traced here: 36.4 us
  Pallas kernels  25.8 us (70%)
  local copies, waits for them, and re-layouts  9.94 us (27%)
  between operations  0.66 us (2%)
    pallas_call x1, Pallas kernels, body(): pl.pallas_call(functools.partial(kernel, nlat, nlon, K, R, C), out_shape=...  25.8 us
    unnamed x17, local copies, waits for them, and re-layouts  9.94 us

profile of v1, /device:TPU:0, one launch (start us, length us, event | category | flops | bytes accessed | tf_op | source)
XLA Modules:
  0.0 36.4 jit_solution(1757910347803299553)
XLA Ops:
  0.6 0.0 copy-start
  0.6 1.7 %copy-done = f32[4,10,64,256]{3,2,1,0:T(8,128)S(1)} copy-done((f32[4,10,64,256]{3,2,1,0:T(8,128)S(1)}, f32[4,10,64,256]{3,2,1,0:T(8,128)}, u32[]{:S(2)}) %copy-start) | copy-done | bytes 2621464
  2.4 0.0 copy-start.1
  2.4 0.8 %copy-done.1 = f32[64,256]{1,0:T(8,128)S(1)} copy-done((f32[64,256]{1,0:T(8,128)S(1)}, f32[64,256]{1,0:T(8,128)}, u32[]{:S(2)}) %copy-start.1) | copy-done | bytes 65560
  3.2 0.0 copy-start.2
  3.2 0.8 %copy-done.2 = f32[64,256]{1,0:T(8,128)S(1)} copy-done((f32[64,256]{1,0:T(8,128)S(1)}, f32[64,256]{1,0:T(8,128)}, u32[]{:S(2)}) %copy-start.2) | copy-done | bytes 65560
  4.1 0.0 copy-start.3
  4.1 0.8 %copy-done.3 = f32[64,256]{1,0:T(8,128)S(1)} copy-done((f32[64,256]{1,0:T(8,128)S(1)}, f32[64,256]{1,0:T(8,128)}, u32[]{:S(2)}) %copy-start.3) | copy-done | bytes 65560
  4.9 0.0 copy-start.4
  4.9 0.8 %copy-done.4 = s32[64,256]{1,0:T(8,128)S(1)} copy-done((s32[64,256]{1,0:T(8,128)S(1)}, s32[64,256]{1,0:T(8,128)}, u32[]{:S(2)}) %copy-start.4) | copy-done | bytes 65560
  5.7 0.0 copy-start.5
  5.7 0.8 %copy-done.5 = s32[64,256]{1,0:T(8,128)S(1)} copy-done((s32[64,256]{1,0:T(8,128)S(1)}, s32[64,256]{1,0:T(8,128)}, u32[]{:S(2)}) %copy-start.5) | copy-done | bytes 65560
  6.6 25.8 %shard_map.101 = (f32[4,10,64,256]{3,2,1,0:T(8,128)S(1)}, f32[64,256]{1,0:T(8,128)S(1)}, f32[64,256]{1,0:T(8,128)S(1)}, f32[64,256]{1,0:T(8,128)S(1)}, f32[64,256]{1,0:T(8,128)S(1)}) custom-call(f32[4,10,64,256]{3,2,1,0:T(8,128)S(1)} %copy-done, f32[64,256]{1,0:T(8,128)S(1)} %copy-done.1, f32[64,256]{1,0:T(8,128)S(1)} %copy-done.2, f32[64,256]{1,0:T(8,128)S(1)} %copy-done.3, ...), custom_call_target="tpu_custom_call" | custom-call | flops 40000000 | bytes 5242880 | tf_op jit(solution)/shard_map/pallas_call | solution.py:474
  32.3 1.5 %copy.16 = f32[4,10,64,256]{3,2,1,0:T(8,128)} copy(f32[4,10,64,256]{3,2,1,0:T(8,128)S(1)} %get-tuple-element.10) | data formatting | bytes 5242880
  33.8 0.6 %copy.17 = f32[64,256]{1,0:T(8,128)} copy(f32[64,256]{1,0:T(8,128)S(1)} %get-tuple-element.11) | data formatting | bytes 131072
  34.5 0.6 %copy.18 = f32[64,256]{1,0:T(8,128)} copy(f32[64,256]{1,0:T(8,128)S(1)} %get-tuple-element.12) | data formatting | bytes 131072
  35.1 0.6 %copy.19 = f32[64,256]{1,0:T(8,128)} copy(f32[64,256]{1,0:T(8,128)S(1)} %get-tuple-element.13) | data formatting | bytes 131072
  35.7 0.6 %copy.20 = f32[64,256]{1,0:T(8,128)} copy(f32[64,256]{1,0:T(8,128)S(1)} %get-tuple-element.14) | data formatting | bytes 131072
Async XLA Ops:
  0.6 1.7 %copy-start = (f32[4,10,64,256]{3,2,1,0:T(8,128)S(1)}, f32[4,10,64,256]{3,2,1,0:T(8,128)}, u32[]{:S(2)}) copy-start(f32[4,10,64,256]{3,2,1,0:T(8,128)} %st_hbm.1) | copy-start | bytes 7864324
  2.4 0.8 %copy-start.1 = (f32[64,256]{1,0:T(8,128)S(1)}, f32[64,256]{1,0:T(8,128)}, u32[]{:S(2)}) copy-start(f32[64,256]{1,0:T(8,128)} %s_hbm.1) | copy-start | bytes 196612
  3.2 0.8 %copy-start.2 = (f32[64,256]{1,0:T(8,128)S(1)}, f32[64,256]{1,0:T(8,128)}, u32[]{:S(2)}) copy-start(f32[64,256]{1,0:T(8,128)} %u_hbm.1) | copy-start | bytes 196612
  4.1 0.8 %copy-start.3 = (f32[64,256]{1,0:T(8,128)S(1)}, f32[64,256]{1,0:T(8,128)}, u32[]{:S(2)}) copy-start(f32[64,256]{1,0:T(8,128)} %v_hbm.1) | copy-start | bytes 196612
  4.9 0.8 %copy-start.4 = (s32[64,256]{1,0:T(8,128)S(1)}, s32[64,256]{1,0:T(8,128)}, u32[]{:S(2)}) copy-start(s32[64,256]{1,0:T(8,128)} %mask_hbm.1) | copy-start | bytes 196612
  5.7 0.8 %copy-start.5 = (s32[64,256]{1,0:T(8,128)S(1)}, s32[64,256]{1,0:T(8,128)}, u32[]{:S(2)}) copy-start(s32[64,256]{1,0:T(8,128)} %lev_hbm.1) | copy-start | bytes 196612

commit v2 on v1

--- a/solution.py
+++ b/solution.py
@@ -463,6 +463,17 @@
         copy.wait_send()
 
 
+def hand_over(*refs):
+    half = len(refs) // 2
+    copies = [
+        pltpu.make_async_copy(refs[i], refs[half + i], refs[-1].at[i]) for i in range(half)
+    ]
+    for copy in copies:
+        copy.start()
+    for copy in copies:
+        copy.wait()
+
+
 def body(ocean_state, surface_height, zonal_transport, meridional_transport, land_mask, levels):
     nlat, nlon = lax.axis_size("lat"), lax.axis_size("lon")
     _, K, R, C = ocean_state.shape
@@ -471,7 +482,9 @@
     pack = -(-(3 * K + 1) // 8) * 8
     vm = lambda *shape: pltpu.VMEM(shape, F32)
     dma = lambda n: pltpu.SemaphoreType.DMA((n,))
-    return pl.pallas_call(
+    args = (ocean_state, surface_height, zonal_transport, meridional_transport, land_mask, levels)
+    args = [pltpu.with_memory_space_constraint(x, pltpu.HBM) for x in args]
+    results = pl.pallas_call(
         functools.partial(kernel, nlat, nlon, K, R, C),
         out_shape=(jax.ShapeDtypeStruct(ocean_state.shape, F32), plane, plane, plane, plane),
         in_specs=[pl.BlockSpec(memory_space=pltpu.HBM)] * 6,
@@ -494,7 +507,14 @@
         cost_estimate=pl.CostEstimate(
             flops=40_000_000, bytes_accessed=2 * ocean_state.size * 4, transcendentals=0
         ),
-    )(ocean_state, surface_height, zonal_transport, meridional_transport, land_mask, levels)
+    )(*args)
+    return pl.pallas_call(
+        hand_over,
+        out_shape=tuple(pltpu.HBM(x.shape, x.dtype) for x in results),
+        in_specs=[pl.BlockSpec(memory_space=pltpu.VMEM)] * 5,
+        out_specs=(pl.BlockSpec(memory_space=pltpu.HBM),) * 5,
+        scratch_shapes=[dma(5)],
+    )(*results)
 
 
 def solution(mesh):

time: 36.7 us -> 35.4 us (0.965)
  local copies, waits for them, and re-layouts: 9.94 us -> 3.98 us
  Pallas kernels: 25.8 us -> 30.6 us
    unnamed x17 -> x10, local copies, waits for them, and re-layouts: 9.94 us -> 3.98 us
    pallas_call x0 -> x1, Pallas kernels: none -> 3.42 us  [body(): pl.pallas_call(hand_over, out_shape=tuple((pltpu.HBM(x.shape, x.dtype) fo...]
    pallas_call x1, Pallas kernels: 25.8 us -> 27.2 us  [body(): pl.pallas_call(functools.partial(kernel, nlat, nlon, K, R, C), out_shape=...]
where the time goes in v2:
time: 35.4 us; the launch traced here: 35.3 us
  Pallas kernels  30.6 us (86%)
  local copies, waits for them, and re-layouts  3.98 us (11%)
  between operations  0.65 us (2%)
    pallas_call x1, Pallas kernels, body(): pl.pallas_call(functools.partial(kernel, nlat, nlon, K, R, C), out_shape=...  27.2 us
    unnamed x10, local copies, waits for them, and re-layouts  3.98 us
    pallas_call x1, Pallas kernels, body(): pl.pallas_call(hand_over, out_shape=tuple((pltpu.HBM(x.shape, x.dtype) fo...  3.42 us

profile of v2, /device:TPU:0, one launch (start us, length us, event | category | flops | bytes accessed | tf_op | source)
XLA Modules:
  0.0 35.3 jit_solution(1049050842031235583)
XLA Ops:
  0.6 27.2 %shard_map.101 = (f32[4,10,64,256]{3,2,1,0:T(8,128)S(1)}, f32[64,256]{1,0:T(8,128)S(1)}, f32[64,256]{1,0:T(8,128)S(1)}, f32[64,256]{1,0:T(8,128)S(1)}, f32[64,256]{1,0:T(8,128)S(1)}) custom-call(f32[4,10,64,256]{3,2,1,0:T(8,128)} %st_hbm.1, f32[64,256]{1,0:T(8,128)} %s_hbm.1, f32[64,256]{1,0:T(8,128)} %u_hbm.1, f32[64,256]{1,0:T(8,128)} %v_hbm.1, ...), custom_call_target="tpu_custom_call" | custom-call | flops 40000000 | bytes 5242880 | tf_op jit(solution)/shard_map/pallas_call | solution.py:487
  27.9 0.0 copy-start
  27.9 1.5 %copy-done = f32[4,10,64,256]{3,2,1,0:T(8,128)} copy-done((f32[4,10,64,256]{3,2,1,0:T(8,128)}, f32[4,10,64,256]{3,2,1,0:T(8,128)S(1)}, u32[]{:S(2)}) %copy-start) | copy-done | bytes 2621464
  29.4 0.0 copy-start.1
  29.4 0.6 %copy-done.1 = f32[64,256]{1,0:T(8,128)} copy-done((f32[64,256]{1,0:T(8,128)}, f32[64,256]{1,0:T(8,128)S(1)}, u32[]{:S(2)}) %copy-start.1) | copy-done | bytes 65560
  30.0 0.0 copy-start.2
  30.0 0.6 %copy-done.2 = f32[64,256]{1,0:T(8,128)} copy-done((f32[64,256]{1,0:T(8,128)}, f32[64,256]{1,0:T(8,128)S(1)}, u32[]{:S(2)}) %copy-start.2) | copy-done | bytes 65560
  30.6 0.0 copy-start.3
  30.6 0.6 %copy-done.3 = f32[64,256]{1,0:T(8,128)} copy-done((f32[64,256]{1,0:T(8,128)}, f32[64,256]{1,0:T(8,128)S(1)}, u32[]{:S(2)}) %copy-start.3) | copy-done | bytes 65560
  31.2 0.0 copy-start.4
  31.2 0.6 %copy-done.4 = f32[64,256]{1,0:T(8,128)} copy-done((f32[64,256]{1,0:T(8,128)}, f32[64,256]{1,0:T(8,128)S(1)}, u32[]{:S(2)}) %copy-start.4) | copy-done | bytes 65560
  31.8 3.4 %shard_map.102 = (f32[4,10,64,256]{3,2,1,0:T(8,128)}, f32[64,256]{1,0:T(8,128)}, f32[64,256]{1,0:T(8,128)}, f32[64,256]{1,0:T(8,128)}, f32[64,256]{1,0:T(8,128)}) custom-call(f32[4,10,64,256]{3,2,1,0:T(8,128)} %copy-done, f32[64,256]{1,0:T(8,128)} %copy-done.1, f32[64,256]{1,0:T(8,128)} %copy-done.2, f32[64,256]{1,0:T(8,128)} %copy-done.3, f32[64,256]{1,0:T(8,128)} %copy-done.4), custom_call_target="tpu_custom_call" | custom-call | tf_op jit(solution)/shard_map/pallas_call | solution.py:511
Async XLA Ops:
  27.9 1.5 %copy-start = (f32[4,10,64,256]{3,2,1,0:T(8,128)}, f32[4,10,64,256]{3,2,1,0:T(8,128)S(1)}, u32[]{:S(2)}) copy-start(f32[4,10,64,256]{3,2,1,0:T(8,128)S(1)} %get-tuple-element.10.refs_0_) | copy-start | bytes 7864324
  29.4 0.6 %copy-start.1 = (f32[64,256]{1,0:T(8,128)}, f32[64,256]{1,0:T(8,128)S(1)}, u32[]{:S(2)}) copy-start(f32[64,256]{1,0:T(8,128)S(1)} %get-tuple-element.11.refs_1_) | copy-start | bytes 196612
  30.0 0.6 %copy-start.2 = (f32[64,256]{1,0:T(8,128)}, f32[64,256]{1,0:T(8,128)S(1)}, u32[]{:S(2)}) copy-start(f32[64,256]{1,0:T(8,128)S(1)} %get-tuple-element.12.refs_2_) | copy-start | bytes 196612
  30.6 0.6 %copy-start.3 = (f32[64,256]{1,0:T(8,128)}, f32[64,256]{1,0:T(8,128)S(1)}, u32[]{:S(2)}) copy-start(f32[64,256]{1,0:T(8,128)S(1)} %get-tuple-element.13.refs_3_) | copy-start | bytes 196612
  31.2 0.6 %copy-start.4 = (f32[64,256]{1,0:T(8,128)}, f32[64,256]{1,0:T(8,128)S(1)}, u32[]{:S(2)}) copy-start(f32[64,256]{1,0:T(8,128)S(1)} %get-tuple-element.14.refs_4_) | copy-start | bytes 196612

commit v3 on v2

--- a/solution.py
+++ b/solution.py
@@ -514,7 +514,8 @@
         in_specs=[pl.BlockSpec(memory_space=pltpu.VMEM)] * 5,
         out_specs=(pl.BlockSpec(memory_space=pltpu.HBM),) * 5,
         scratch_shapes=[dma(5)],
-    )(*results)
+        compiler_params=pltpu.CompilerParams(vmem_limit_bytes=4 * 1024 * 1024),
+    )(*[pltpu.with_memory_space_constraint(x, pltpu.VMEM) for x in results])
 
 
 def solution(mesh):

time: 35.4 us -> 29.6 us (0.84)
  local copies, waits for them, and re-layouts: 3.98 us -> 0 us
  Pallas kernels: 30.6 us -> 28.8 us
    unnamed x10 -> x0, local copies, waits for them, and re-layouts: 3.98 us -> none
    pallas_call x1, Pallas kernels: 3.42 us -> 1.6 us  [body(): pl.pallas_call(hand_over, out_shape=tuple((pltpu.HBM(x.shape, x.dtype) fo...]
where the time goes in v3:
time: 29.6 us; the launch traced here: 29.5 us
  Pallas kernels  28.8 us (97%)
  between operations  0.64 us (2%)
    pallas_call x1, Pallas kernels, body(): pl.pallas_call(functools.partial(kernel, nlat, nlon, K, R, C), out_shape=...  27.2 us
    pallas_call x1, Pallas kernels, body(): pl.pallas_call(hand_over, out_shape=tuple((pltpu.HBM(x.shape, x.dtype) fo...  1.6 us

profile of v3, /device:TPU:0, one launch (start us, length us, event | category | flops | bytes accessed | tf_op | source)
XLA Modules:
  0.0 29.5 jit_solution(17185409829376558382)
XLA Ops:
  0.6 27.2 %shard_map.101 = (f32[4,10,64,256]{3,2,1,0:T(8,128)S(1)}, f32[64,256]{1,0:T(8,128)S(1)}, f32[64,256]{1,0:T(8,128)S(1)}, f32[64,256]{1,0:T(8,128)S(1)}, f32[64,256]{1,0:T(8,128)S(1)}) custom-call(f32[4,10,64,256]{3,2,1,0:T(8,128)} %st_hbm.1, f32[64,256]{1,0:T(8,128)} %s_hbm.1, f32[64,256]{1,0:T(8,128)} %u_hbm.1, f32[64,256]{1,0:T(8,128)} %v_hbm.1, ...), custom_call_target="tpu_custom_call" | custom-call | flops 40000000 | bytes 5242880 | tf_op jit(solution)/shard_map/pallas_call | solution.py:487
  27.9 1.6 %shard_map.102 = (f32[4,10,64,256]{3,2,1,0:T(8,128)}, f32[64,256]{1,0:T(8,128)}, f32[64,256]{1,0:T(8,128)}, f32[64,256]{1,0:T(8,128)}, f32[64,256]{1,0:T(8,128)}) custom-call(f32[4,10,64,256]{3,2,1,0:T(8,128)S(1)} %get-tuple-element.10.refs_0_, f32[64,256]{1,0:T(8,128)S(1)} %get-tuple-element.11.refs_1_, f32[64,256]{1,0:T(8,128)S(1)} %get-tuple-element.12.refs_2_, ...), custom_call_target="tpu_custom_call" | custom-call | tf_op jit(solution)/shard_map/pallas_call | solution.py:511

commit v4 on v3

--- a/solution.py
+++ b/solution.py
@@ -46,7 +46,7 @@
     ns, os_ref, ou_ref, ov_ref, op_ref,
     ts, uv, pr, ml, w, le, ln, fw0, fs0,
     pcw, pce, re, rw, pkn, pks, rn, rs, fold1, fold4, foldf,
-    c2w, c2e, r2e, r2w, ae, an, dd, gg, tot, totr,
+    c2w, c2e, r2e, r2w, ae, an, dd, gg, tot, tot2, totr,
     lsem, ssem, rsem, tssem, trsem,
 ):
     lat, lon = lax.axis_index("lat"), lax.axis_index("lon")
@@ -150,7 +150,7 @@
             pce[rr, :] = b
         return tuple(out)
 
-    lax.fori_loop(0, K, pressure_level, tuple(jnp.zeros((CH, C), F32) for _ in chunks))
+    lax.fori_loop(0, K, pressure_level, tuple(jnp.zeros((CH, C), F32) for _ in chunks), unroll=2)
     for k in range(K):
         pkn[k : k + 1, :] = ts[0, k, R - 1 : R, :]
         pkn[K + k : K + k + 1, :] = ts[1, k, R - 1 : R, :]
@@ -249,7 +249,7 @@
             return fx + gx * thick, fy + gy * thick
 
         zero = jnp.zeros((CH, C), F32)
-        fx, fy = lax.fori_loop(0, K, force_level, (zero, zero))
+        fx, fy = lax.fori_loop(0, K, force_level, (zero, zero), unroll=5)
         w[4, c0 + r : c0 + r + CH, 0:C] = 0.1 * fx
         w[5, c0 + r : c0 + r + CH, 0:C] = 0.1 * fy
 
@@ -436,7 +436,7 @@
     low_tri = (iota((R, R), 0) >= iota((R, R), 1)).astype(F32)
     zonal = w[1, c0:c1, 0:C]
     op_ref[...] = exact_dot(low_tri, zonal)
-    tot[...] = jnp.broadcast_to(op_ref[R - 1 : R, :], tot.shape)
+    tot[...] = op_ref[R - 1 : R, :]
     sends = []
     for d in range(1, nlat):
         sends.append(
@@ -445,20 +445,32 @@
                 {"lat": lax.rem(lat + d, nlat)},
             )
         )
-    for send in sends:
-        send.start()
+    for d in range(nlat - 1, 0, -1):
+
+        @pl.when(lat + d < nlat)
+        def _():
+            sends[d - 1].start()
+
     lax.fori_loop(second, K, tracer_level, 0)
     os_ref[...] = w[0, c0:c1, 0:C]
     ou_ref[...] = zonal
     ov_ref[...] = w[2, c0:c1, 0:C]
-    south = jnp.zeros((8, C), F32)
+    tot2[...] = jnp.zeros(tot2.shape, F32)
     for d in range(1, nlat):
-        sends[d - 1].wait_recv()
-        south = south + totr[d - 1] * (lat >= d).astype(F32)
+
+        @pl.when(lat >= d)
+        def _():
+            sends[d - 1].wait_recv()
+            tot2[...] = tot2[...] + totr[d - 1]
+
     scale = -1.0 / math.sqrt(R * nlat)
-    op_ref[...] = (op_ref[...] + south[0:1, :]) * scale
-    for send in sends:
-        send.wait_send()
+    op_ref[...] = (op_ref[...] + tot2[...]) * scale
+    for d in range(1, nlat):
+
+        @pl.when(lat + d < nlat)
+        def _():
+            sends[d - 1].wait_send()
+
     for copy in (col_w, col_e, far_w, far_e):
         copy.wait_send()
 
@@ -498,7 +510,7 @@
             vm(4, RIM, C), vm(2, RIM, C),
             vm(wide[0], LANES), vm(wide[0], LANES), vm(wide[0], LANES), vm(wide[0], LANES),
             vm(*wide), vm(*wide), vm(RIM, wide[1]), vm(RIM, wide[1]),
-            vm(8, C), vm(nlat - 1, 8, C),
+            vm(1, C), vm(1, C), vm(nlat - 1, 1, C),
             dma(7), dma(10), dma(10), dma(nlat - 1), dma(nlat - 1),
         ],
         compiler_params=pltpu.CompilerParams(

time: 29.6 us -> 22.7 us (0.77)
  the two profiles are of different devices: /device:TPU:0 before, /device:TPU:25 now
where the time goes in v4:
time: 22.7 us; the launch traced here: 22.5 us
  Pallas kernels  21.9 us (96%)
  between operations  0.64 us (3%)
    pallas_call x1, Pallas kernels, body(): pl.pallas_call(functools.partial(kernel, nlat, nlon, K, R, C), out_shape=...  20.3 us
    pallas_call x1, Pallas kernels, body(): pl.pallas_call(hand_over, out_shape=tuple((pltpu.HBM(x.shape, x.dtype) fo...  1.6 us

profile of v4, /device:TPU:25, one launch (start us, length us, event | category | flops | bytes accessed | tf_op | source)
XLA Modules:
  0.0 22.5 jit_solution(10359568961777151236)
XLA Ops:
  0.6 20.3 %shard_map.101 = (f32[4,10,64,256]{3,2,1,0:T(8,128)S(1)}, f32[64,256]{1,0:T(8,128)S(1)}, f32[64,256]{1,0:T(8,128)S(1)}, f32[64,256]{1,0:T(8,128)S(1)}, f32[64,256]{1,0:T(8,128)S(1)}) custom-call(f32[4,10,64,256]{3,2,1,0:T(8,128)} %st_hbm.1, f32[64,256]{1,0:T(8,128)} %s_hbm.1, f32[64,256]{1,0:T(8,128)} %u_hbm.1, f32[64,256]{1,0:T(8,128)} %v_hbm.1, ...), custom_call_target="tpu_custom_call" | custom-call | flops 40000000 | bytes 5242880 | tf_op jit(solution)/shard_map/pallas_call | solution.py:499
  20.9 1.6 %shard_map.102 = (f32[4,10,64,256]{3,2,1,0:T(8,128)}, f32[64,256]{1,0:T(8,128)}, f32[64,256]{1,0:T(8,128)}, f32[64,256]{1,0:T(8,128)}, f32[64,256]{1,0:T(8,128)}) custom-call(f32[4,10,64,256]{3,2,1,0:T(8,128)S(1)} %get-tuple-element.10.refs_0_, f32[64,256]{1,0:T(8,128)S(1)} %get-tuple-element.11.refs_1_, f32[64,256]{1,0:T(8,128)S(1)} %get-tuple-element.12.refs_2_, ...), custom_call_target="tpu_custom_call" | custom-call | tf_op jit(solution)/shard_map/pallas_call | solution.py:523

commit v5 on v4

--- a/solution.py
+++ b/solution.py
@@ -150,7 +150,7 @@
             pce[rr, :] = b
         return tuple(out)
 
-    lax.fori_loop(0, K, pressure_level, tuple(jnp.zeros((CH, C), F32) for _ in chunks), unroll=2)
+    lax.fori_loop(0, K, pressure_level, tuple(jnp.zeros((CH, C), F32) for _ in chunks), unroll=5)
     for k in range(K):
         pkn[k : k + 1, :] = ts[0, k, R - 1 : R, :]
         pkn[K + k : K + k + 1, :] = ts[1, k, R - 1 : R, :]
@@ -249,7 +249,7 @@
             return fx + gx * thick, fy + gy * thick
 
         zero = jnp.zeros((CH, C), F32)
-        fx, fy = lax.fori_loop(0, K, force_level, (zero, zero), unroll=5)
+        fx, fy = lax.fori_loop(0, K, force_level, (zero, zero), unroll=10)
         w[4, c0 + r : c0 + r + CH, 0:C] = 0.1 * fx
         w[5, c0 + r : c0 + r + CH, 0:C] = 0.1 * fy
 
@@ -431,7 +431,7 @@
         dd[...] = dd[...] - gg[...]
         return carry
 
-    lax.fori_loop(1, NSUB, substep, 0)
+    lax.fori_loop(1, NSUB, substep, 0, unroll=3)
 
     low_tri = (iota((R, R), 0) >= iota((R, R), 1)).astype(F32)
     zonal = w[1, c0:c1, 0:C]

time: 22.7 us -> 21.8 us (0.960)
  the two profiles are of different devices: /device:TPU:25 before, /device:TPU:24 now
where the time goes in v5:
time: 21.8 us; the launch traced here: 21.7 us
  Pallas kernels  21 us (96%)
  between operations  0.64 us (3%)
    pallas_call x1, Pallas kernels, body(): pl.pallas_call(functools.partial(kernel, nlat, nlon, K, R, C), out_shape=...  19.4 us
    pallas_call x1, Pallas kernels, body(): pl.pallas_call(hand_over, out_shape=tuple((pltpu.HBM(x.shape, x.dtype) fo...  1.6 us

profile of v5, /device:TPU:24, one launch (start us, length us, event | category | flops | bytes accessed | tf_op | source)
XLA Modules:
  0.0 21.7 jit_solution(6489628631195055018)
XLA Ops:
  0.6 19.4 %shard_map.101 = (f32[4,10,64,256]{3,2,1,0:T(8,128)S(1)}, f32[64,256]{1,0:T(8,128)S(1)}, f32[64,256]{1,0:T(8,128)S(1)}, f32[64,256]{1,0:T(8,128)S(1)}, f32[64,256]{1,0:T(8,128)S(1)}) custom-call(f32[4,10,64,256]{3,2,1,0:T(8,128)} %st_hbm.1, f32[64,256]{1,0:T(8,128)} %s_hbm.1, f32[64,256]{1,0:T(8,128)} %u_hbm.1, f32[64,256]{1,0:T(8,128)} %v_hbm.1, ...), custom_call_target="tpu_custom_call" | custom-call | flops 40000000 | bytes 5242880 | tf_op jit(solution)/shard_map/pallas_call | solution.py:499
  20.1 1.6 %shard_map.102 = (f32[4,10,64,256]{3,2,1,0:T(8,128)}, f32[64,256]{1,0:T(8,128)}, f32[64,256]{1,0:T(8,128)}, f32[64,256]{1,0:T(8,128)}, f32[64,256]{1,0:T(8,128)}) custom-call(f32[4,10,64,256]{3,2,1,0:T(8,128)S(1)} %get-tuple-element.10.refs_0_, f32[64,256]{1,0:T(8,128)S(1)} %get-tuple-element.11.refs_1_, f32[64,256]{1,0:T(8,128)S(1)} %get-tuple-element.12.refs_2_, ...), custom_call_target="tpu_custom_call" | custom-call | tf_op jit(solution)/shard_map/pallas_call | solution.py:523
